TPU v7x, 256 devices: a whole 4x4x8 slice. The times are simulated.
256 devices in a mesh: rep: 4 (over y), exp: 16 (over z, core), tp: 4 (over x).
Axes of the slice: x: 4, y: 4, z: 8, core: 2. Of those that a mesh axis runs over, the one named last changes fastest.
Arguments:
- tokens: bfloat16 [8192, 4096], P(('rep', 'exp'), 'tp'), may hold values from -6 to 6
- expert_id: int32 [8192, 1], P(('rep', 'exp')), may hold values from 0 to 15; in each aligned block of 128 rows (0 to 127, 128 to 255, ...) at most 32 rows name the same one
- route_weight: float32 [8192, 1], P(('rep', 'exp')), may hold values from 0.1 to 0.6
- cluster_id: int32 [128], replicated, may hold values from 0 to 3
- out_grad: bfloat16 [8192, 4096], P(('rep', 'exp'), 'tp'), may hold values from -6 to 6
- w_gate: bfloat16 [16, 4096, 1536], P('exp', None, 'tp'), may hold values from -0.09375 to 0.09375
- w_up: bfloat16 [16, 4096, 1536], P('exp', None, 'tp'), may hold values from -0.09375 to 0.09375
- w_down: bfloat16 [16, 1536, 4096], P('exp', 'tp'), may hold values from -0.15625 to 0.15625
Outputs:
- mixed: bfloat16 [8192, 4096], P(('rep', 'exp'), 'tp')
- grad_tokens: bfloat16 [8192, 4096], P(('rep', 'exp'), 'tp')
- grad_gate: bfloat16 [16, 4096, 1536], P('exp', 'rep', 'tp')
- grad_up: bfloat16 [16, 4096, 1536], P('exp', 'rep', 'tp')
- grad_down: bfloat16 [16, 1536, 4096], P('exp', 'tp', 'rep')
Inputs may be any that keep to these rules, and one draw needn't show every extreme that they name: `expert_id`: in each aligned block of 128 tokens (the tokens held by one (rep, exp) position) no expert is named by more than 32 routes, and in every draw some block names some expert exactly 32 times.
All inputs are finite; a program needn't handle non-finite values.
Results may differ from a plain program's by a relative error of at most 0.015.
Values may be sent and summed in bfloat16 or wider, within the bound.
A program may use at most 128 MiB of HBM per device.

v0:
```python
import jax
import jax.numpy as jnp
from jax import lax
from jax.sharding import PartitionSpec as P

TOP = 1
ROLL_DEV = 2
GROUP = 16


def vote_advantage(cluster_id):
    total_rollouts = cluster_id.shape[0]
    group_of = jnp.arange(total_rollouts, dtype=jnp.int32) // GROUP
    same_vote = (cluster_id[:, None] == cluster_id[None, :]) & (
        group_of[:, None] == group_of[None, :]
    )
    agreement = jnp.sum(same_vote.astype(jnp.float32), axis=1)
    group_mean = jnp.mean(agreement.reshape(total_rollouts // GROUP, GROUP), axis=1)
    return agreement - jnp.repeat(group_mean, GROUP)


def contract_rows(left_mat, right_mat):
    return lax.dot_general(
        left_mat, right_mat, (((0,), (0,)), ((), ())), preferred_element_type=jnp.float32
    )


def contract_cols(left_mat, right_mat):
    return lax.dot_general(
        left_mat, right_mat, (((1,), (1,)), ((), ())), preferred_element_type=jnp.float32
    )


def body(tokens, expert_id, route_weight, cluster_id, out_grad, w_gate, w_up, w_down):
    token_count = tokens.shape[0]
    experts = lax.axis_size("exp")
    capacity = min(token_count, 4 * token_count * TOP // experts)
    slot_count = experts * capacity
    shard_index = lax.axis_index("rep") * experts + lax.axis_index("exp")
    advantage = vote_advantage(cluster_id)
    own_advantage = lax.dynamic_slice_in_dim(advantage, shard_index * ROLL_DEV, ROLL_DEV)
    token_advantage = jnp.repeat(own_advantage, token_count // ROLL_DEV)
    weight = route_weight[:, 0]
    cotangent = ((token_advantage * weight)[:, None] * out_grad.astype(jnp.float32)).astype(
        jnp.bfloat16
    )
    expert_ids = expert_id[:, 0]
    onehot = (expert_ids[:, None] == jnp.arange(experts, dtype=jnp.int32)[None, :]).astype(
        jnp.int32
    )
    slot_rank = jnp.sum((jnp.cumsum(onehot, axis=0) - 1) * onehot, axis=1)
    slot_of = expert_ids * capacity + slot_rank
    source = (
        jnp.full((slot_count,), token_count, jnp.int32)
        .at[slot_of]
        .set(jnp.arange(token_count, dtype=jnp.int32))
    )
    zero_row = jnp.zeros((1, tokens.shape[1]), jnp.bfloat16)
    send_tokens = jnp.concatenate([tokens, zero_row], axis=0)[source].reshape(experts, capacity, -1)
    send_cot = jnp.concatenate([cotangent, zero_row], axis=0)[source].reshape(experts, capacity, -1)
    got_tokens, got_cot = (
        lax.all_to_all(send_tokens, "exp", split_axis=0, concat_axis=0, tiled=True),
        lax.all_to_all(send_cot, "exp", split_axis=0, concat_axis=0, tiled=True),
    )
    full_tokens, full_cot = (
        lax.all_gather(got_tokens, "tp", axis=2, tiled=True),
        lax.all_gather(got_cot, "tp", axis=2, tiled=True),
    )
    row_tokens = full_tokens.reshape(slot_count, -1)
    row_cot = full_cot.reshape(slot_count, -1)
    gate_mat = w_gate[0]
    up_mat = w_up[0]
    down_mat = w_down[0]
    hidden_width = gate_mat.shape[1]
    pre_gate = jnp.dot(row_tokens, gate_mat, preferred_element_type=jnp.float32)
    pre_up = jnp.dot(row_tokens, up_mat, preferred_element_type=jnp.float32)
    sigmoid_gate = jax.nn.sigmoid(pre_gate)
    silu_gate = pre_gate * sigmoid_gate
    hidden = (silu_gate * pre_up).astype(jnp.bfloat16)
    partial_out = jnp.dot(hidden, down_mat, preferred_element_type=jnp.float32)
    grad_hidden = contract_cols(row_cot, down_mat)
    grad_pre_gate = (
        grad_hidden * pre_up * sigmoid_gate * (1.0 + pre_gate * (1.0 - sigmoid_gate))
    ).astype(jnp.bfloat16)
    grad_pre_up = (grad_hidden * silu_gate).astype(jnp.bfloat16)
    partial_in = contract_cols(grad_pre_gate, gate_mat) + contract_cols(grad_pre_up, up_mat)
    out_sum, in_sum = (
        lax.psum_scatter(
            partial_out.astype(jnp.bfloat16), "tp", scatter_dimension=1, tiled=True
        ).astype(jnp.float32),
        lax.psum_scatter(
            partial_in.astype(jnp.bfloat16), "tp", scatter_dimension=1, tiled=True
        ).astype(jnp.float32),
    )
    returned_out, returned_grad = (
        lax.all_to_all(
            out_sum.astype(jnp.bfloat16).reshape(experts, capacity, -1),
            "exp",
            split_axis=0,
            concat_axis=0,
            tiled=True,
        ),
        lax.all_to_all(
            in_sum.astype(jnp.bfloat16).reshape(experts, capacity, -1),
            "exp",
            split_axis=0,
            concat_axis=0,
            tiled=True,
        ),
    )
    token_out = returned_out.reshape(slot_count, -1)[slot_of]
    mixed = (weight[:, None] * token_out.astype(jnp.float32)).astype(jnp.bfloat16)
    grad_tokens = returned_grad.reshape(slot_count, -1)[slot_of]
    summed = lax.psum_scatter(
        jnp.concatenate(
            [
                contract_rows(row_tokens, grad_pre_gate),
                contract_rows(row_tokens, grad_pre_up),
                contract_rows(row_cot, hidden),
            ],
            axis=1,
        ).astype(jnp.bfloat16),
        "rep",
        scatter_dimension=0,
        tiled=True,
    ).astype(jnp.float32)
    gate_sum = summed[:, :hidden_width]
    up_sum = summed[:, hidden_width : 2 * hidden_width]
    down_sum = summed[:, 2 * hidden_width :]
    grad_gate = gate_sum.astype(jnp.bfloat16)[None]
    grad_up = up_sum.astype(jnp.bfloat16)[None]
    grad_down = down_sum.T.astype(jnp.bfloat16)[None]
    return (mixed, grad_tokens, grad_gate, grad_up, grad_down)


def solution(mesh):
    placed = (
        P(("rep", "exp"), "tp"),
        P(("rep", "exp"), None),
        P(("rep", "exp"), None),
        P(),
        P(("rep", "exp"), "tp"),
        P("exp", None, "tp"),
        P("exp", None, "tp"),
        P("exp", "tp", None),
    )
    return jax.shard_map(
        body,
        mesh=mesh,
        in_specs=placed,
        out_specs=(
            P(("rep", "exp"), "tp"),
            P(("rep", "exp"), "tp"),
            P("exp", "rep", "tp"),
            P("exp", "rep", "tp"),
            P("exp", "tp", "rep"),
        ),
        check_vma=False,
    )
```

profile of v0, /device:TPU:9, one launch (start us, length us, event | category | flops | bytes accessed | tf_op | source)
XLA Modules:
  0.0 374.4 jit_solution(14382489026064247872)
XLA Ops:
  7.2 0.9 fusion.11
  8.3 0.8 select_reduce_fusion
  9.8 1.0 scatter_custom_fusion
  10.8 1.0 concatenate.10
  11.8 2.8 gather_fusion
  14.6 37.8 %all_to_all.20 = bf16[16,32,1024]{2,1,0:T(8,128)(2,1)} all-to-all(bf16[16,32,1024]{2,1,0:T(8,128)(2,1)} %bitcast.58), channel_id=1, replica_groups=mesh['rep'=4,'exp'=16,'tp'=4] {'exp'}, dimensions={0} | all-to-all | bytes 2097152 | tf_op jit(solution)/shard_map/all_to_all | solution.py:62
  53.3 1.1 multiply_convert_fusion.3
  54.4 2.8 gather_fusion.2
  57.2 31.5 %all_to_all.21 = bf16[16,32,1024]{2,1,0:T(8,128)(2,1)} all-to-all(bf16[16,32,1024]{2,1,0:T(8,128)(2,1)} %bitcast.57), channel_id=1, replica_groups=mesh['rep'=4,'exp'=16,'tp'=4] {'exp'}, dimensions={0} | all-to-all | bytes 2097152 | tf_op jit(solution)/shard_map/all_to_all | solution.py:63
  88.7 11.2 %all-gather.3.cloned.1.call-done = bf16[16,32,4096]{2,1,0:T(8,128)(2,1)} async-done(((bf16[16,32,1024]{2,1,0:T(8,128)(2,1)}), bf16[16,32,4096]{2,1,0:T(8,128)(2,1)}) %all-gather.3.cloned.1.call-update) | async-done | bytes 4194320 | tf_op jit(solution)/shard_map/all_gather | solution.py:66
  100.0 6.5 %fusion.4 = f32[512,384]{1,0:T(8,128)} fusion(bf16[512,4096]{1,0:T(8,128)(2,1)} %bitcast.64, bf16[1,4096,384]{2,1,0:T(8,128)(2,1)} %param.14), kind=kOutput, calls=%fused_computation.15 | convolution fusion | flops 1610612736 | bytes 8126464 | tf_op jit(solution)/shard_map/dot_general | solution.py:76
  106.5 3.2 fusion.8
  109.7 43.3 %all-gather.5.cloned.1.call-done = bf16[16,32,4096]{2,1,0:T(8,128)(2,1)} async-done(((bf16[16,32,1024]{2,1,0:T(8,128)(2,1)}), bf16[16,32,4096]{2,1,0:T(8,128)(2,1)}) %all-gather.5.cloned.1.call-update) | async-done | bytes 4194320 | tf_op jit(solution)/shard_map/all_gather | solution.py:67
  153.0 6.1 %multiply_convert_fusion = (bf16[512,384]{1,0:T(8,128)(2,1)S(1)}, bf16[512,384]{1,0:T(8,128)(2,1)S(1)}, bf16[512,384]{1,0:T(8,128)(2,1)}) fusion(f32[512,384]{1,0:T(8,128)} %fusion.8, f32[512,384]{1,0:T(8,128)} %fusion.4, bf16[512,4096]{1,0:T(8,128)(2,1)} %bitcast.68, bf16[1,384,4096]{2,1,0:T(8,128)(2,1)S(1)} %copy-done), kind=kOutput, calls=%fused_computation.24 | convolution fusion | flops 1613561856 | bytes 10092544 | tf_op jit(solution)/shard_map/dot_general | solution.py:29
  159.1 2.4 fusion.6
  161.5 4.5 %add_convert_fusion = bf16[512,4096]{1,0:T(8,128)(2,1)} fusion(f32[512,4096]{1,0:T(8,128)S(1)} %fusion.6, bf16[512,384]{1,0:T(8,128)(2,1)S(1)} %get-tuple-element.18, bf16[1,4096,384]{2,1,0:T(8,128)(2,1)S(1)} %copy-done.4), kind=kOutput, calls=%fused_computation.6 | convolution fusion | flops 1614807040 | bytes 16121856 | tf_op jit(solution)/shard_map/dot_general | solution.py:29
  166.2 5.3 %convolution_convert_fusion = bf16[512,4096]{1,0:T(8,128)(2,1)} fusion(bf16[512,384]{1,0:T(8,128)(2,1)} %get-tuple-element.20, bf16[1,384,4096]{2,1,0:T(8,128)(2,1)S(1)} %copy-done), kind=kOutput, calls=%fused_computation.7 | convolution fusion | flops 1612709888 | bytes 7733248 | tf_op jit(solution)/shard_map/dot_general | solution.py:80
  171.5 4.2 %convolution_convert_fusion.1 = bf16[4096,384]{0,1:T(8,128)(2,1)S(1)} fusion(bf16[512,4096]{1,0:T(8,128)(2,1)} %bitcast.69, bf16[512,384]{1,0:T(8,128)(2,1)} %get-tuple-element.20), kind=kOutput, calls=%fused_computation.8 | convolution fusion | flops 1612185600 | bytes 7733248 | tf_op jit(solution)/shard_map/dot_general | solution.py:23
  175.8 1.9 convolution_convert_fusion.2
  177.7 1.8 convolution_convert_fusion.3
  179.5 4.3 %pad_maximum_fusion = bf16[4096,1152]{0,1:T(8,128)(2,1)} fusion(bf16[4096,384]{0,1:T(8,128)(2,1)S(1)} %convolution_convert_fusion.1, bf16[4096,384]{0,1:T(8,128)(2,1)S(1)} %convolution_convert_fusion.2, bf16[4096,384]{0,1:T(8,128)(2,1)S(1)} %convolution_convert_fusion.3), kind=kLoop, calls=%fused_computation.5 | loop fusion | flops 28311552 | bytes 18874368 | tf_op jit(solution)/shard_map/concatenate | solution.py:115
  183.9 32.0 %reduce-scatter.6.cloned.1.call-done = bf16[512,1024]{1,0:T(8,128)(2,1)} async-done(((bf16[512,4096]{1,0:T(8,128)(2,1)}), bf16[512,1024]{1,0:T(8,128)(2,1)}) %reduce-scatter.6.cloned.1.call-update) | async-done | bytes 1048592 | tf_op jit(solution)/shard_map/reduce_scatter | solution.py:91
  215.9 7.7 %all-to-all-start.3 = ((bf16[16,32,1024]{2,1,0:T(8,128)(2,1)}), bf16[16,32,1024]{2,1,0:T(8,128)(2,1)S(1)}, u32[]{:S(2)}, u32[]{:S(2)}) async-start(bf16[16,32,1024]{2,1,0:T(8,128)(2,1)} %bitcast.60), calls=%async_computation.5 | async-start | bytes 2097152 | tf_op jit(solution)/shard_map/all_to_all | solution.py:103
  223.6 44.1 %reduce-scatter.4.cloned.1.call-done = bf16[512,1024]{1,0:T(8,128)(2,1)} async-done(((bf16[512,4096]{1,0:T(8,128)(2,1)}), bf16[512,1024]{1,0:T(8,128)(2,1)}) %reduce-scatter.4.cloned.1.call-update) | async-done | bytes 1048592 | tf_op jit(solution)/shard_map/reduce_scatter | solution.py:88
  267.6 7.6 %all-to-all-start.1 = ((bf16[16,32,1024]{2,1,0:T(8,128)(2,1)}), bf16[16,32,1024]{2,1,0:T(8,128)(2,1)S(1)}, u32[]{:S(2)}, u32[]{:S(2)}) async-start(bf16[16,32,1024]{2,1,0:T(8,128)(2,1)} %bitcast.59), calls=%async_computation.2 | async-start | bytes 2097152 | tf_op jit(solution)/shard_map/all_to_all | solution.py:96
  275.3 1.6 gather_fusion.3
  276.8 26.4 %all-to-all-done.1 = bf16[16,32,1024]{2,1,0:T(8,128)(2,1)S(1)} async-done(((bf16[16,32,1024]{2,1,0:T(8,128)(2,1)}), bf16[16,32,1024]{2,1,0:T(8,128)(2,1)S(1)}, u32[]{:S(2)}, u32[]{:S(2)}) %all-to-all-start.1) | async-done | bytes 1048608 | tf_op jit(solution)/shard_map/all_to_all | solution.py:96
  303.2 0.9 gather_fusion.1
  304.9 55.3 %reduce-scatter.8.cloned.1.call-done = bf16[1024,1152]{0,1:T(8,128)(2,1)} async-done(((bf16[4096,1152]{0,1:T(8,128)(2,1)}), bf16[1024,1152]{0,1:T(8,128)(2,1)}) %reduce-scatter.8.cloned.1.call-update) | async-done | bytes 2359312 | tf_op jit(solution)/shard_map/reduce_scatter | solution.py:114
  360.2 3.1 slice_bitcast_fusion
  363.2 2.3 copy.15
  365.5 2.3 copy.16
  (53 shorter events, 3.0 us)
Async XLA Ops:
  7.2 145.8 %copy-start = (bf16[1,384,4096]{2,1,0:T(8,128)(2,1)S(1)}, bf16[1,384,4096]{2,1,0:T(8,128)(2,1)}, u32[]{:S(2)}) copy-start(bf16[1,384,4096]{2,1,0:T(8,128)(2,1)} %param.15) | copy-start | bytes 9437188
  7.2 92.8 %all-gather.3.cloned.1.call-start = ((), (), s32[]{:S(2)}) async-start(), calls=%async_computation.7 | async-start | bytes 5242880 | tf_op jit(solution)/shard_map/all_gather | solution.py:66
  11.8 40.7 %copy-start.7 = (s32[128]{0:T(128)S(1)}, s32[128]{0:T(128)}, u32[]{:S(2)}) copy-start(s32[128]{0:T(128)} %param.11) | copy-start | bytes 1540
  11.8 41.5 %copy-start.8 = (f32[128,1]{0,1:T(1,128)S(1)}, f32[128,1]{0,1:T(1,128)}, u32[]{:S(2)}) copy-start(f32[128,1]{0,1:T(1,128)} %param.10) | copy-start | bytes 1540
  52.4 100.6 %all-gather.5.cloned.1.call-start = ((), (), s32[]{:S(2)}) async-start(), calls=%async_computation.9 | async-start | bytes 5242880 | tf_op jit(solution)/shard_map/all_gather | solution.py:67
  88.7 127.2 %reduce-scatter.6.cloned.1.call-start = ((), (), s32[]{:S(2)}) async-start(), calls=%async_computation.10 | async-start | bytes 5242880 | tf_op jit(solution)/shard_map/reduce_scatter | solution.py:91
  100.0 6.5 %copy-start.2 = (bf16[1,4096,384]{2,1,0:T(8,128)(2,1)S(1)}, bf16[1,4096,384]{2,1,0:T(8,128)(2,1)}, u32[]{:S(2)}) copy-start(bf16[1,4096,384]{2,1,0:T(8,128)(2,1)} %param.13) | copy-start | bytes 9437188
  100.0 6.5 %copy-start.9 = (bf16[16,32,4096]{2,1,0:T(8,128)(2,1)S(1)}, bf16[16,32,4096]{2,1,0:T(8,128)(2,1)}, u32[]{:S(2)}) copy-start(bf16[16,32,4096]{2,1,0:T(8,128)(2,1)} %all-gather.3.cloned.1.call-done) | copy-start | bytes 12582916
  153.0 6.1 %copy-start.3 = (bf16[1,4096,384]{2,1,0:T(8,128)(2,1)S(1)}, bf16[1,4096,384]{2,1,0:T(8,128)(2,1)}, u32[]{:S(2)}) copy-start(bf16[1,4096,384]{2,1,0:T(8,128)(2,1)} %param.13) | copy-start | bytes 9437188
  159.1 2.4 copy-start.5
  159.1 2.4 copy-start.4
  165.9 101.7 %reduce-scatter.4.cloned.1.call-start = ((), (), s32[]{:S(2)}) async-start(), calls=%async_computation.8 | async-start | bytes 5242880 | tf_op jit(solution)/shard_map/reduce_scatter | solution.py:88
  171.5 188.7 %reduce-scatter.8.cloned.1.call-start = ((), (), s32[]{:S(2)}) async-start(), calls=%async_computation.11 | async-start | bytes 11796480 | tf_op jit(solution)/shard_map/reduce_scatter | solution.py:114
  171.5 4.3 %copy-start.6 = (bf16[512,384]{1,0:T(8,128)(2,1)S(1)}, bf16[512,384]{1,0:T(8,128)(2,1)}, u32[]{:S(2)}) copy-start(bf16[512,384]{1,0:T(8,128)(2,1)} %copy-done.5) | copy-start | bytes 1179652
  171.5 4.3 %copy-start.10 = (bf16[16,32,4096]{2,1,0:T(8,128)(2,1)S(1)}, bf16[16,32,4096]{2,1,0:T(8,128)(2,1)}, u32[]{:S(2)}) copy-start(bf16[16,32,4096]{2,1,0:T(8,128)(2,1)} %all-gather.3.cloned.1.call-done) | copy-start | bytes 12582916
  215.9 51.7 %all-to-all-start.3 = ((bf16[16,32,1024]{2,1,0:T(8,128)(2,1)}), bf16[16,32,1024]{2,1,0:T(8,128)(2,1)S(1)}, u32[]{:S(2)}, u32[]{:S(2)}) async-start(bf16[16,32,1024]{2,1,0:T(8,128)(2,1)} %bitcast.60), calls=%async_computation.5 | async-start | bytes 2097152 | tf_op jit(solution)/shard_map/all_to_all | solution.py:103
  267.6 35.6 %all-to-all-start.1 = ((bf16[16,32,1024]{2,1,0:T(8,128)(2,1)}), bf16[16,32,1024]{2,1,0:T(8,128)(2,1)S(1)}, u32[]{:S(2)}, u32[]{:S(2)}) async-start(bf16[16,32,1024]{2,1,0:T(8,128)(2,1)} %bitcast.59), calls=%async_computation.2 | async-start | bytes 2097152 | tf_op jit(solution)/shard_map/all_to_all | solution.py:96
  304.0 63.8 %copy-start.1 = (bf16[1,384,4096]{2,1,0:T(8,128)(2,1)S(1)}, bf16[1,384,4096]{2,1,0:T(8,128)(2,1)}, u32[]{:S(2)}) copy-start(bf16[1,384,4096]{2,1,0:T(8,128)(2,1)} %param.15) | copy-start | bytes 9437188
Sparse Core Ops, SparseCore 0:
  52.5 47.4 all-gather.2
  101.8 51.1 all-gather.4
  166.1 49.7 reduce-scatter.5
  218.5 49.1 reduce-scatter.3
  270.1 90.0 reduce-scatter.7
where the time goes:
time: 377 us; the launch traced here: 374 us
  waiting for transfers between devices  212 us (56%)
  blocking collectives  69.3 us (18%)
  matrix products  35.8 us (9%)
  local copies, waits for them, and re-layouts  18.1 us (5%)
  starting transfers between devices  15.7 us (4%)
  between operations  14 us (4%)
  other arithmetic  9.07 us (2%)
    reduce_scatter x1, waiting for transfers between devices, body(): lax.psum_scatter(jnp.concatenate([contract_rows(row_tokens, grad_pre_gate...  55.3 us
    reduce_scatter x1, waiting for transfers between devices, body(): lax.psum_scatter(partial_out.astype(jnp.bfloat16), 'tp', scatter_dimensio...  44.1 us
    all_gather x1, waiting for transfers between devices, body(): lax.all_gather(got_cot, 'tp', axis=2, tiled=True)  43.3 us
    all_to_all x1, blocking collectives, body(): lax.all_to_all(send_tokens, 'exp', split_axis=0, concat_axis=0, tiled=True)  37.8 us
    reduce_scatter x1, waiting for transfers between devices, body(): lax.psum_scatter(partial_in.astype(jnp.bfloat16), 'tp', scatter_dimension...  32 us
    all_to_all x1, blocking collectives, body(): lax.all_to_all(send_cot, 'exp', split_axis=0, concat_axis=0, tiled=True)  31.5 us
    all_to_all x1, waiting for transfers between devices, body(): lax.all_to_all(out_sum.astype(jnp.bfloat16).reshape(experts, capacity, -1...  26.4 us
    dot_general x3, matrix products, contract_cols(): lax.dot_general(left_mat, right_mat, (((1,), (1,)), ((), ())), preferred_...  12.9 us
  transfers between devices with their start and end apart: 7, of which 6 were waited for; matrix products, arithmetic and copies ran while one was open for 9% of the time, Pallas kernels for 0%

commit v1 on v0

v1 whole, which is shorter than its diff:
```python
import jax
import jax.numpy as jnp
from jax import lax
from jax.experimental import pallas as pl
from jax.experimental.pallas import tpu as pltpu
from jax.sharding import PartitionSpec as P

MESH = pl.DeviceIdType.MESH
F32, BF16 = jnp.float32, jnp.bfloat16
TOK = 128
CAP = 32
NE = 16
ROWS = NE * CAP
FB = 1024
HID = 384
GROUP = 16
CH = 4
CROWS = ROWS // CH
HALVES = 2
HROWS = ROWS // HALVES
QROWS = HROWS // 2
FAR = (0, 1, 7, 2, 6, 3, 5, 4)


def dot_nn(a, b):
    return lax.dot_general(a, b, (((1,), (0,)), ((), ())), preferred_element_type=F32)


def dot_nt(a, b):
    return lax.dot_general(a, b, (((1,), (1,)), ((), ())), preferred_element_type=F32)


def dot_tn(a, b):
    return lax.dot_general(a, b, (((0,), (0,)), ((), ())), preferred_element_type=F32)


def kernel(
    tokens,
    eid_col,
    eid_row,
    weight,
    clu_col,
    clu_row,
    out_grad,
    w_gate,
    w_up,
    w_down,
    mixed,
    grad_tokens,
    out_gate,
    out_up,
    out_down,
    send_t,
    send_c,
    rows_t,
    rows_c,
    wg,
    wu,
    wd,
    slope,
    silu,
    hidden,
    gpre,
    part_o,
    x_one,
    x_left,
    x_right,
    ret,
    g_gu,
    g_dn,
    y_one_gu,
    y_one_dn,
    y_left_gu,
    y_left_dn,
    y_right_gu,
    y_right_dn,
    w_sem,
    z_ssem,
    z_rsem,
    ag_ssem,
    ag_rsem,
    rs_ssem,
    rs_rsem,
    zr_ssem,
    zr_rsem,
    y_ssem,
    y_rsem,
):
    x, y, e = lax.axis_index("tp"), lax.axis_index("rep"), lax.axis_index("exp")
    z, core = e // 2, e % 2
    x_next, x_prev = {"tp": (x + 1) % 4}, {"tp": (x + 3) % 4}
    y_next, y_prev = {"rep": (y + 1) % 4}, {"rep": (y + 3) % 4}

    def to_of(j):
        return {"exp": ((z + FAR[j // 2]) % 8) * 2 + (core + j % 2) % 2}

    def from_of(j):
        return {"exp": ((z + 8 - FAR[j // 2]) % 8) * 2 + (core + j % 2) % 2}

    sends = []

    def remote(src, dst, ssem, rsem, where):
        return pltpu.make_async_remote_copy(
            src_ref=src,
            dst_ref=dst,
            send_sem=ssem,
            recv_sem=rsem,
            device_id=where,
            device_id_type=MESH,
        )

    loads = []
    for i in range(4):
        at = pl.ds(pl.multiple_of(((x + i) % 4) * FB, FB), FB)
        loads.append(pltpu.make_async_copy(w_gate.at[0, at, :], wg.at[i], w_sem.at[i]))
        loads.append(pltpu.make_async_copy(w_up.at[0, at, :], wu.at[i], w_sem.at[4 + i]))
        loads.append(pltpu.make_async_copy(w_down.at[0, :, at], wd.at[i], w_sem.at[8 + i]))
    for load in loads:
        load.start()

    barrier = pltpu.get_barrier_semaphore()
    for where in [to_of(j) for j in range(1, NE)] + [x_next, x_prev, y_next, y_prev]:
        pl.semaphore_signal(barrier, inc=1, device_id=where, device_id_type=MESH)

    def place(ids):
        away = ((ids >> 1) - z + 8) & 7
        first = jnp.where(away == 0, 0, jnp.where(away <= 4, 2 * away - 1, 16 - 2 * away))
        return (2 * first + (((ids & 1) + core) & 1)) * CAP

    ids_col, ids_row = eid_col[...], eid_row[...]
    sub = lax.broadcasted_iota(jnp.int32, (TOK, TOK), 0)
    lane = lax.broadcasted_iota(jnp.int32, (TOK, TOK), 1)
    same = ids_col == ids_row
    rank_col = jnp.sum(jnp.where(same & (lane < sub), 1.0, 0.0), axis=1, keepdims=True)
    rank_row = jnp.sum(jnp.where(same & (sub < lane), 1.0, 0.0), axis=0, keepdims=True)
    slot_col = place(ids_col) + rank_col.astype(jnp.int32)
    slot_row = place(ids_row) + rank_row.astype(jnp.int32)
    pick = jnp.where(
        lax.broadcasted_iota(jnp.int32, (ROWS, TOK), 0) == slot_row, 1.0, 0.0
    ).astype(BF16)
    send_t[...] = dot_nn(pick, tokens[...]).astype(BF16)

    pl.semaphore_wait(barrier, NE - 1 + 4)

    def z_copy(k, j):
        src, dst = ((send_t, rows_t), (send_c, rows_c))[k]
        at = pl.ds(j * CAP, CAP)
        return remote(src.at[at], dst.at[0, at], z_ssem.at[k, j], z_rsem.at[k, j], to_of(j))

    for j in range(1, NE):
        z_copy(0, j).start()
    rows_t[0, 0:CAP, :] = send_t[0:CAP, :]

    same_group = (sub // GROUP) == (lane // GROUP)
    votes = jnp.where((clu_col[...] == clu_row[...]) & same_group, 1.0, 0.0)
    agree_row = jnp.sum(votes, axis=0, keepdims=True)
    agree_col = jnp.sum(votes, axis=1, keepdims=True)
    mean_row = jnp.sum(jnp.where(same_group, agree_col, 0.0), axis=0, keepdims=True) * (1.0 / GROUP)
    own = 2 * (y * NE + e) + sub // (TOK // 2)
    adv = jnp.sum(jnp.where(lane == own, agree_row - mean_row, 0.0), axis=1, keepdims=True)
    cot = ((adv * weight[...]) * out_grad[...].astype(F32)).astype(BF16)
    send_c[...] = dot_nn(pick, cot).astype(BF16)
    for j in range(1, NE):
        z_copy(1, j).start()
    rows_c[0, 0:CAP, :] = send_c[0:CAP, :]

    def ag_copies(k, c):
        buf = (rows_t, rows_c)[k]
        lo = pl.ds(c * CROWS, CROWS)
        a = pl.ds(c * CROWS, CROWS // 2)
        b = pl.ds(c * CROWS + CROWS // 2, CROWS // 2)
        s, r = ag_ssem, ag_rsem
        return (
            remote(buf.at[0, lo], buf.at[3, lo], s.at[k, c, 0], r.at[k, c, 0], x_next),
            remote(buf.at[0, lo], buf.at[1, lo], s.at[k, c, 1], r.at[k, c, 1], x_prev),
            remote(buf.at[3, a], buf.at[2, a], s.at[k, c, 2], r.at[k, c, 2], x_next),
            remote(buf.at[1, b], buf.at[2, b], s.at[k, c, 3], r.at[k, c, 3], x_prev),
        )

    def ag_send(k, c):
        for j in range(max(4 * c, 1), 4 * c + 4):
            z_copy(k, j).wait_recv()
        for copy in ag_copies(k, c)[:2]:
            copy.start()

    def ag_forward(k, c):
        copies = ag_copies(k, c)
        copies[0].wait_recv()
        copies[2].start()
        copies[1].wait_recv()
        copies[3].start()

    def ag_wait(k, c):
        for copy in ag_copies(k, c)[2:]:
            copy.wait_recv()

    def hrows(m):
        return pl.ds(m * HROWS, HROWS)

    def first_layer(m):
        at = hrows(m)
        pre_g = dot_nn(rows_t[0, at, :], wg[0])
        for i in range(1, 4):
            pre_g += dot_nn(rows_t[i, at, :], wg[i])
        slope[at, :] = pre_g
        pre_u = dot_nn(rows_t[0, at, :], wu[0])
        for i in range(1, 4):
            pre_u += dot_nn(rows_t[i, at, :], wu[i])
        pre_g = slope[at, :]
        sig = jax.nn.sigmoid(pre_g)
        act = pre_g * sig
        hidden[at, :] = (act * pre_u).astype(BF16)
        silu[at, :] = act
        slope[at, :] = pre_u * sig * (1.0 + pre_g * (1.0 - sig))

    def second_layer(m):
        @pl.loop(0, 4)
        def _(i):
            part_o[i, hrows(m), :] = dot_nn(hidden[hrows(m), :], wd[i]).astype(BF16)

    def back_hidden(m):
        at = hrows(m)
        grad = dot_nt(rows_c[0, at, :], wd[0])
        for i in range(1, 4):
            grad += dot_nt(rows_c[i, at, :], wd[i])
        gpre[at, 0:HID] = (grad * slope[at, :]).astype(BF16)
        gpre[at, HID:] = (grad * silu[at, :]).astype(BF16)

    part_i = rows_t

    def back_tokens(m):
        @pl.loop(0, 4)
        def _(i):
            part_i[i, hrows(m), :] = (
                dot_nt(gpre[hrows(m), 0:HID], wg[i]) + dot_nt(gpre[hrows(m), HID:], wu[i])
            ).astype(BF16)

    ORDER = (2, 1, 3, 0)

    def weight_grads(k):
        i = (y + ORDER[k] - x + 4) % 4

        @pl.loop(0, 4)
        def _(f):
            at = pl.ds(pl.multiple_of(f * 256, 256), 256)
            g_gu[k, at, :] = dot_tn(rows_t[i, :, at], gpre[...]).astype(BF16)
            g_dn[k, :, at] = dot_tn(hidden[...], rows_c[i, :, at]).astype(BF16)

    def rs_copies(k, m):
        part = (part_o, part_i)[k]
        a, b = pl.ds(m * HROWS, QROWS), pl.ds(m * HROWS + QROWS, QROWS)
        s, r = rs_ssem, rs_rsem
        return (
            remote(part.at[2, a], x_one.at[k, m, 0], s.at[k, m, 0], r.at[k, m, 0], x_next),
            remote(part.at[2, b], x_one.at[k, m, 1], s.at[k, m, 1], r.at[k, m, 1], x_prev),
            remote(part.at[1, b], x_left.at[k, b], s.at[k, m, 2], r.at[k, m, 2], x_next),
            remote(part.at[3, a], x_right.at[k, a], s.at[k, m, 3], r.at[k, m, 3], x_prev),
            remote(part.at[1, a], x_left.at[k, a], s.at[k, m, 4], r.at[k, m, 4], x_next),
            remote(part.at[3, b], x_right.at[k, b], s.at[k, m, 5], r.at[k, m, 5], x_prev),
        )

    def add_into(ref, at, other):
        ref[at] = (ref[at].astype(F32) + other.astype(F32)).astype(BF16)

    def rs_first(k):
        for m in range(HALVES):
            for copy in rs_copies(k, m)[:2]:
                copy.start()
        for m in range(HALVES):
            for copy in rs_copies(k, m)[2:4]:
                copy.start()

    def rs_pass_on(k, m):
        part = (part_o, part_i)[k]
        copies = rs_copies(k, m)
        copies[0].wait_recv()
        add_into(part, (1, pl.ds(m * HROWS, QROWS)), x_one[k, m, 0])
        copies[4].start()
        copies[1].wait_recv()
        add_into(part, (3, pl.ds(m * HROWS + QROWS, QROWS)), x_one[k, m, 1])
        copies[5].start()

    total = (send_t, send_c)

    def zr_copy(k, j):
        at = pl.ds(j * CAP, CAP)
        return remote(
            total[k].at[at], ret.at[k, at], zr_ssem.at[k, j], zr_rsem.at[k, j], from_of(j)
        )

    def rs_last(k, m):
        part = (part_o, part_i)[k]
        for copy in rs_copies(k, m)[2:]:
            copy.wait_recv()
        at = hrows(m)
        total[k][at, :] = (
            part[0, at, :].astype(F32)
            + x_left[k, at, :].astype(F32)
            + x_right[k, at, :].astype(F32)
        ).astype(BF16)
        for j in reversed(range(max(m * 8, 1), m * 8 + 8)):
            zr_copy(k, j).start()
        if m == 0:
            ret[k, 0:CAP, :] = total[k][0:CAP, :]

    def back(k):
        for j in range(1, NE):
            zr_copy(k, j).wait_recv()
        spread = jnp.where(
            lax.broadcasted_iota(jnp.int32, (TOK, ROWS), 1) == slot_col, 1.0, 0.0
        ).astype(BF16)
        return dot_nn(spread, ret[k])

    def y_copies():
        s, r = y_ssem, y_rsem
        gu_a, gu_b = pl.ds(0, FB // 2), pl.ds(FB // 2, FB // 2)
        dn_a, dn_b = pl.ds(0, HID // 2), pl.ds(HID // 2, HID // 2)
        return (
            (
                remote(g_gu.at[0, gu_a], y_one_gu.at[0], s.at[0], r.at[0], y_next),
                remote(g_dn.at[0, dn_a], y_one_dn.at[0], s.at[1], r.at[1], y_next),
                remote(g_gu.at[0, gu_b], y_one_gu.at[1], s.at[2], r.at[2], y_prev),
                remote(g_dn.at[0, dn_b], y_one_dn.at[1], s.at[3], r.at[3], y_prev),
            ),
            (
                remote(g_gu.at[1, gu_b], y_left_gu.at[gu_b], s.at[4], r.at[4], y_next),
                remote(g_dn.at[1, dn_b], y_left_dn.at[dn_b], s.at[5], r.at[5], y_next),
            ),
            (
                remote(g_gu.at[2, gu_a], y_right_gu.at[gu_a], s.at[6], r.at[6], y_prev),
                remote(g_dn.at[2, dn_a], y_right_dn.at[dn_a], s.at[7], r.at[7], y_prev),
            ),
            (
                remote(g_gu.at[1, gu_a], y_left_gu.at[gu_a], s.at[8], r.at[8], y_next),
                remote(g_dn.at[1, dn_a], y_left_dn.at[dn_a], s.at[9], r.at[9], y_next),
                remote(g_gu.at[2, gu_b], y_right_gu.at[gu_b], s.at[10], r.at[10], y_prev),
                remote(g_dn.at[2, dn_b], y_right_dn.at[dn_b], s.at[11], r.at[11], y_prev),
            ),
        )

    ag_send(0, 0)
    ag_send(0, 1)
    ag_forward(0, 0)
    ag_send(0, 2)
    ag_forward(0, 1)
    ag_send(0, 3)
    ag_forward(0, 2)
    ag_send(1, 0)
    ag_forward(0, 3)
    ag_send(1, 1)
    for load in loads:
        load.wait()
    ag_wait(0, 0)
    ag_wait(0, 1)
    first_layer(0)
    ag_send(1, 2)
    ag_forward(1, 0)
    ag_send(1, 3)
    ag_wait(0, 2)
    ag_wait(0, 3)
    first_layer(1)
    ag_forward(1, 1)
    second_layer(0)
    second_layer(1)
    ag_forward(1, 2)
    ag_wait(1, 0)
    ag_wait(1, 1)
    back_hidden(0)
    ag_forward(1, 3)
    rs_first(0)
    ag_wait(1, 2)
    ag_wait(1, 3)
    back_hidden(1)
    ys = y_copies()
    weight_grads(0)
    for copy in ys[0]:
        copy.start()
    weight_grads(1)
    for copy in ys[1]:
        copy.start()
    weight_grads(2)
    for copy in ys[2]:
        copy.start()
    rs_pass_on(0, 0)
    rs_pass_on(0, 1)
    weight_grads(3)
    for c in range(CH):
        for copy in ag_copies(0, c):
            copy.wait_send()
    back_tokens(0)
    back_tokens(1)
    rs_first(1)
    for k in range(2):
        for j in range(1, NE):
            z_copy(k, j).wait_send()
    rs_last(0, 0)
    for copy in ys[0]:
        copy.wait_recv()
    FH, HH = FB // 2, HID // 2
    add_into(g_gu, (1, pl.ds(0, FH)), y_one_gu[0])
    add_into(g_dn, (1, pl.ds(0, HH)), y_one_dn[0])
    ys[3][0].start()
    ys[3][1].start()
    add_into(g_gu, (2, pl.ds(FH, FH)), y_one_gu[1])
    add_into(g_dn, (2, pl.ds(HH, HH)), y_one_dn[1])
    ys[3][2].start()
    ys[3][3].start()
    rs_last(0, 1)
    rs_pass_on(1, 0)
    rs_pass_on(1, 1)
    rs_last(1, 0)
    rs_last(1, 1)
    mixed[...] = (weight[...] * back(0).astype(BF16).astype(F32)).astype(BF16)
    for copy in ys[1] + ys[2] + ys[3]:
        copy.wait_recv()
    both = (
        g_gu[3].astype(F32) + y_left_gu[...].astype(F32) + y_right_gu[...].astype(F32)
    ).astype(BF16)
    out_gate[0] = both[:, :HID]
    out_up[0] = both[:, HID:]
    out_down[0] = (
        g_dn[3].astype(F32) + y_left_dn[...].astype(F32) + y_right_dn[...].astype(F32)
    ).astype(BF16)
    grad_tokens[...] = back(1).astype(BF16)

    for c in range(CH):
        for copy in ag_copies(1, c):
            copy.wait_send()
    for k in range(2):
        for m in range(HALVES):
            for copy in rs_copies(k, m):
                copy.wait_send()
        for j in range(1, NE):
            zr_copy(k, j).wait_send()
    for group in ys:
        for copy in group:
            copy.wait_send()


def body(tokens, expert_id, route_weight, cluster_id, out_grad, w_gate, w_up, w_down):
    vmem, far = pl.BlockSpec(memory_space=pltpu.VMEM), pl.BlockSpec(memory_space=pl.ANY)
    dma = pltpu.SemaphoreType.DMA
    rollouts = cluster_id.shape[0]
    return pl.pallas_call(
        kernel,
        out_shape=(
            jax.ShapeDtypeStruct((TOK, FB), BF16),
            jax.ShapeDtypeStruct((TOK, FB), BF16),
            jax.ShapeDtypeStruct((1, FB, HID), BF16),
            jax.ShapeDtypeStruct((1, FB, HID), BF16),
            jax.ShapeDtypeStruct((1, HID, FB), BF16),
        ),
        in_specs=[vmem] * 7 + [far] * 3,
        out_specs=(vmem,) * 5,
        scratch_shapes=[
            pltpu.VMEM((ROWS, FB), BF16),
            pltpu.VMEM((ROWS, FB), BF16),
            pltpu.VMEM((4, ROWS, FB), BF16),
            pltpu.VMEM((4, ROWS, FB), BF16),
            pltpu.VMEM((4, FB, HID), BF16),
            pltpu.VMEM((4, FB, HID), BF16),
            pltpu.VMEM((4, HID, FB), BF16),
            pltpu.VMEM((ROWS, HID), F32),
            pltpu.VMEM((ROWS, HID), F32),
            pltpu.VMEM((ROWS, HID), BF16),
            pltpu.VMEM((ROWS, 2 * HID), BF16),
            pltpu.VMEM((4, ROWS, FB), BF16),
            pltpu.VMEM((2, HALVES, 2, QROWS, FB), BF16),
            pltpu.VMEM((2, ROWS, FB), BF16),
            pltpu.VMEM((2, ROWS, FB), BF16),
            pltpu.VMEM((2, ROWS, FB), BF16),
            pltpu.VMEM((4, FB, 2 * HID), BF16),
            pltpu.VMEM((4, HID, FB), BF16),
            pltpu.VMEM((2, FB // 2, 2 * HID), BF16),
            pltpu.VMEM((2, HID // 2, FB), BF16),
            pltpu.VMEM((FB, 2 * HID), BF16),
            pltpu.VMEM((HID, FB), BF16),
            pltpu.VMEM((FB, 2 * HID), BF16),
            pltpu.VMEM((HID, FB), BF16),
            dma((12,)),
            dma((2, NE)),
            dma((2, NE)),
            dma((2, CH, 4)),
            dma((2, CH, 4)),
            dma((2, HALVES, 6)),
            dma((2, HALVES, 6)),
            dma((2, NE)),
            dma((2, NE)),
            dma((12,)),
            dma((12,)),
        ],
        compiler_params=pltpu.CompilerParams(
            collective_id=0, has_side_effects=True, vmem_limit_bytes=60 * 2**20
        ),
        name="expert_layer",
    )(
        tokens,
        expert_id,
        expert_id.reshape(1, TOK),
        route_weight,
        cluster_id.reshape(rollouts, 1),
        cluster_id.reshape(1, rollouts),
        out_grad,
        w_gate,
        w_up,
        w_down,
    )


def solution(mesh):
    placed = (
        P(("rep", "exp"), "tp"),
        P(("rep", "exp"), None),
        P(("rep", "exp"), None),
        P(),
        P(("rep", "exp"), "tp"),
        P("exp", None, "tp"),
        P("exp", None, "tp"),
        P("exp", "tp", None),
    )
    return jax.shard_map(
        body,
        mesh=mesh,
        in_specs=placed,
        out_specs=(
            P(("rep", "exp"), "tp"),
            P(("rep", "exp"), "tp"),
            P("exp", "rep", "tp"),
            P("exp", "rep", "tp"),
            P("exp", "tp", "rep"),
        ),
        check_vma=False,
    )
```

time: 377 us -> 194 us (0.51)
  waiting for transfers between devices: 212 us -> 0 us
  Pallas kernels: 0 us -> 180 us
  blocking collectives: 69.3 us -> 0 us
  matrix products: 35.8 us -> 0 us
  starting transfers between devices: 15.7 us -> 0 us
  between operations: 14 us -> 0.66 us
  other arithmetic: 9.07 us -> 0 us
  local copies, waits for them, and re-layouts: 18.1 us -> 11.5 us
    pallas_call x0 -> x1, Pallas kernels: none -> 180 us  [body(): pl.pallas_call(kernel, out_shape=(jax.ShapeDtypeStruct((TOK, FB), BF16),...]
    reduce_scatter x3 -> x0, waiting for transfers between devices: 131 us -> none  [the longest x1 55.3 us: body(): lax.psum_scatter(jnp.concatenate([contract_rows(row_tokens, grad_pre_gate...]
    all_to_all x2 -> x0, blocking collectives: 69.3 us -> none  [the longest x1 37.8 us: body(): lax.all_to_all(send_tokens, 'exp', split_axis=0, concat_axis=0, tiled=True)]
    all_gather x2 -> x0, waiting for transfers between devices: 54.5 us -> none  [the longest x1 43.3 us: body(): lax.all_gather(got_cot, 'tp', axis=2, tiled=True)]
    dot_general x9 -> x0, matrix products: 35.8 us -> none  [the longest x3 12.9 us: contract_cols(): lax.dot_general(left_mat, right_mat, (((1,), (1,)), ((), ())), preferred_...]
    all_to_all x2 -> x0, waiting for transfers between devices: 26.4 us -> none  [the longest x1 26.4 us: body(): lax.all_to_all(out_sum.astype(jnp.bfloat16).reshape(experts, capacity, -1...]
    all_to_all x2 -> x0, starting transfers between devices: 15.3 us -> none  [the longest x1 7.66 us: body(): lax.all_to_all(in_sum.astype(jnp.bfloat16).reshape(experts, capacity, -1)...]
    gather x4 -> x0, local copies, waits for them, and re-layouts: 7.97 us -> none  [the longest x1 2.78 us: body(): jnp.concatenate([cotangent, zero_row], axis=0)[source]]
  transfers between devices with their start and end apart: 7 -> 0, of which waited for: 6 -> 0; matrix products, arithmetic and copies ran while one was open for 9% -> 0% of each run, Pallas kernels for 0% -> 0%
where the time goes in v1:
time: 194 us; the launch traced here: 192 us
  Pallas kernels  180 us (93%)
  local copies, waits for them, and re-layouts  11.5 us (6%)
    pallas_call x1, Pallas kernels, body(): pl.pallas_call(kernel, out_shape=(jax.ShapeDtypeStruct((TOK, FB), BF16),...  180 us
    unnamed x11, local copies, waits for them, and re-layouts  10.1 us

profile of v1, /device:TPU:9, one launch (start us, length us, event | category | flops | bytes accessed | tf_op | source)
XLA Modules:
  0.0 192.4 jit_solution(8971245317135669660)
XLA Ops:
  0.6 1.4 copy.14.weight
  2.0 1.4 copy.15.clu_col
  3.4 1.4 copy.13.eid_col
  4.8 180.3 %expert_layer.1 = (bf16[128,1024]{1,0:T(8,128)(2,1)}, bf16[128,1024]{1,0:T(8,128)(2,1)}, bf16[1,1024,384]{2,1,0:T(8,128)(2,1)}, bf16[1,1024,384]{2,1,0:T(8,128)(2,1)}, bf16[1,384,1024]{2,1,0:T(8,128)(2,1)}) custom-call(bf16[128,1024]{1,0:T(8,128)(2,1)} %tokens.1, s32[128,1]{1,0:T(8,128)} %copy.13.eid_col, s32[1,128]{1,0:T(1,128)} %bitcast.3, ...), custom_call_target="tpu_custom_call" | custom-call | tf_op jit(solution)/shard_map/expert_layer/pallas_call | solution.py:444
  185.1 0.0 copy-start.1
  185.1 0.0 copy-start
  185.1 1.8 copy.21
  186.9 1.7 copy.22
  188.5 2.1 %copy.23 = bf16[1,1024,384]{2,1,0:T(8,128)(2,1)} copy(bf16[1,1024,384]{2,1,0:T(8,128)(2,1)} %get-tuple-element.12) | data formatting | bytes 1572864
  190.6 0.0 copy-done.1
  190.6 0.9 copy.24
  191.5 0.0 copy-done
  191.5 0.9 copy.25
Async XLA Ops:
  185.1 5.6 %copy-start.1 = (bf16[1,1024,384]{2,1,0:T(8,128)(2,1)S(1)}, bf16[1,1024,384]{2,1,0:T(8,128)(2,1)}, u32[]{:S(2)}) copy-start(bf16[1,1024,384]{2,1,0:T(8,128)(2,1)} %get-tuple-element.13) | copy-start | bytes 2359300
  185.1 6.4 %copy-start = (bf16[1,384,1024]{2,1,0:T(8,128)(2,1)S(1)}, bf16[1,384,1024]{2,1,0:T(8,128)(2,1)}, u32[]{:S(2)}) copy-start(bf16[1,384,1024]{2,1,0:T(8,128)(2,1)} %get-tuple-element.14) | copy-start | bytes 2359300

commit v2 on v1

--- a/solution.py
+++ b/solution.py
@@ -14,11 +14,11 @@
 FB = 1024
 HID = 384
 GROUP = 16
+LIMIT = 56
 CH = 4
 CROWS = ROWS // CH
-HALVES = 2
-HROWS = ROWS // HALVES
-QROWS = HROWS // 2
+HROWS = ROWS // 2
+QROWS = CROWS // 2
 FAR = (0, 1, 7, 2, 6, 3, 5, 4)
 
 
@@ -35,13 +35,11 @@
 
 
 def kernel(
-    tokens,
-    eid_col,
     eid_row,
-    weight,
-    clu_col,
+    weight_row,
     clu_row,
-    out_grad,
+    tokens_far,
+    out_grad_far,
     w_gate,
     w_up,
     w_down,
@@ -50,6 +48,8 @@
     out_gate,
     out_up,
     out_down,
+    tokens,
+    out_grad,
     send_t,
     send_c,
     rows_t,
@@ -109,6 +109,14 @@
             device_id_type=MESH,
         )
 
+    barrier = pltpu.get_barrier_semaphore()
+    for where in [to_of(j) for j in range(1, NE)] + [x_next, x_prev, y_next, y_prev]:
+        pl.semaphore_signal(barrier, inc=1, device_id=where, device_id_type=MESH)
+    load_t = pltpu.make_async_copy(tokens_far, tokens, w_sem.at[12])
+    load_t.start()
+    load_c = pltpu.make_async_copy(out_grad_far, out_grad, w_sem.at[13])
+    load_c.start()
+
     loads = []
     for i in range(4):
         at = pl.ds(pl.multiple_of(((x + i) % 4) * FB, FB), FB)
@@ -118,18 +126,19 @@
     for load in loads:
         load.start()
 
-    barrier = pltpu.get_barrier_semaphore()
-    for where in [to_of(j) for j in range(1, NE)] + [x_next, x_prev, y_next, y_prev]:
-        pl.semaphore_signal(barrier, inc=1, device_id=where, device_id_type=MESH)
-
     def place(ids):
         away = ((ids >> 1) - z + 8) & 7
         first = jnp.where(away == 0, 0, jnp.where(away <= 4, 2 * away - 1, 16 - 2 * away))
         return (2 * first + (((ids & 1) + core) & 1)) * CAP
 
-    ids_col, ids_row = eid_col[...], eid_row[...]
     sub = lax.broadcasted_iota(jnp.int32, (TOK, TOK), 0)
     lane = lax.broadcasted_iota(jnp.int32, (TOK, TOK), 1)
+
+    def column(row):
+        return jnp.sum(jnp.where(sub == lane, row, 0), axis=1, keepdims=True)
+
+    ids_row = eid_row[...]
+    ids_col = column(ids_row)
     same = ids_col == ids_row
     rank_col = jnp.sum(jnp.where(same & (lane < sub), 1.0, 0.0), axis=1, keepdims=True)
     rank_row = jnp.sum(jnp.where(same & (sub < lane), 1.0, 0.0), axis=0, keepdims=True)
@@ -138,6 +147,7 @@
     pick = jnp.where(
         lax.broadcasted_iota(jnp.int32, (ROWS, TOK), 0) == slot_row, 1.0, 0.0
     ).astype(BF16)
+    load_t.wait()
     send_t[...] = dot_nn(pick, tokens[...]).astype(BF16)
 
     pl.semaphore_wait(barrier, NE - 1 + 4)
@@ -147,21 +157,25 @@
         at = pl.ds(j * CAP, CAP)
         return remote(src.at[at], dst.at[0, at], z_ssem.at[k, j], z_rsem.at[k, j], to_of(j))
 
-    for j in range(1, NE):
-        z_copy(0, j).start()
+    def z_start(k, c):
+        for j in range(max(4 * c, 1), 4 * c + 4):
+            z_copy(k, j).start()
+
+    z_start(0, 0)
+    z_start(0, 1)
     rows_t[0, 0:CAP, :] = send_t[0:CAP, :]
 
     same_group = (sub // GROUP) == (lane // GROUP)
-    votes = jnp.where((clu_col[...] == clu_row[...]) & same_group, 1.0, 0.0)
+    votes = jnp.where((column(clu_row[...]) == clu_row[...]) & same_group, 1.0, 0.0)
     agree_row = jnp.sum(votes, axis=0, keepdims=True)
     agree_col = jnp.sum(votes, axis=1, keepdims=True)
     mean_row = jnp.sum(jnp.where(same_group, agree_col, 0.0), axis=0, keepdims=True) * (1.0 / GROUP)
     own = 2 * (y * NE + e) + sub // (TOK // 2)
     adv = jnp.sum(jnp.where(lane == own, agree_row - mean_row, 0.0), axis=1, keepdims=True)
-    cot = ((adv * weight[...]) * out_grad[...].astype(F32)).astype(BF16)
+    weight = column(weight_row[...])
+    load_c.wait()
+    cot = ((adv * weight) * out_grad[...].astype(F32)).astype(BF16)
     send_c[...] = dot_nn(pick, cot).astype(BF16)
-    for j in range(1, NE):
-        z_copy(1, j).start()
     rows_c[0, 0:CAP, :] = send_c[0:CAP, :]
 
     def ag_copies(k, c):
@@ -248,7 +262,7 @@
 
     def rs_copies(k, m):
         part = (part_o, part_i)[k]
-        a, b = pl.ds(m * HROWS, QROWS), pl.ds(m * HROWS + QROWS, QROWS)
+        a, b = pl.ds(m * CROWS, QROWS), pl.ds(m * CROWS + QROWS, QROWS)
         s, r = rs_ssem, rs_rsem
         return (
             remote(part.at[2, a], x_one.at[k, m, 0], s.at[k, m, 0], r.at[k, m, 0], x_next),
@@ -262,22 +276,18 @@
     def add_into(ref, at, other):
         ref[at] = (ref[at].astype(F32) + other.astype(F32)).astype(BF16)
 
-    def rs_first(k):
-        for m in range(HALVES):
-            for copy in rs_copies(k, m)[:2]:
-                copy.start()
-        for m in range(HALVES):
-            for copy in rs_copies(k, m)[2:4]:
-                copy.start()
+    def rs_first(k, m):
+        for copy in rs_copies(k, m)[:4]:
+            copy.start()
 
     def rs_pass_on(k, m):
         part = (part_o, part_i)[k]
         copies = rs_copies(k, m)
         copies[0].wait_recv()
-        add_into(part, (1, pl.ds(m * HROWS, QROWS)), x_one[k, m, 0])
+        add_into(part, (1, pl.ds(m * CROWS, QROWS)), x_one[k, m, 0])
         copies[4].start()
         copies[1].wait_recv()
-        add_into(part, (3, pl.ds(m * HROWS + QROWS, QROWS)), x_one[k, m, 1])
+        add_into(part, (3, pl.ds(m * CROWS + QROWS, QROWS)), x_one[k, m, 1])
         copies[5].start()
 
     total = (send_t, send_c)
@@ -292,13 +302,13 @@
         part = (part_o, part_i)[k]
         for copy in rs_copies(k, m)[2:]:
             copy.wait_recv()
-        at = hrows(m)
+        at = pl.ds(m * CROWS, CROWS)
         total[k][at, :] = (
             part[0, at, :].astype(F32)
             + x_left[k, at, :].astype(F32)
             + x_right[k, at, :].astype(F32)
         ).astype(BF16)
-        for j in reversed(range(max(m * 8, 1), m * 8 + 8)):
+        for j in range(max(m * 4, 1), m * 4 + 4):
             zr_copy(k, j).start()
         if m == 0:
             ret[k, 0:CAP, :] = total[k][0:CAP, :]
@@ -339,12 +349,18 @@
         )
 
     ag_send(0, 0)
+    z_start(0, 2)
     ag_send(0, 1)
+    z_start(0, 3)
     ag_forward(0, 0)
     ag_send(0, 2)
+    z_start(1, 0)
+    z_start(1, 1)
     ag_forward(0, 1)
     ag_send(0, 3)
+    z_start(1, 2)
     ag_forward(0, 2)
+    z_start(1, 3)
     ag_send(1, 0)
     ag_forward(0, 3)
     ag_send(1, 1)
@@ -360,14 +376,15 @@
     ag_wait(0, 3)
     first_layer(1)
     ag_forward(1, 1)
+    second_layer(1)
     second_layer(0)
-    second_layer(1)
     ag_forward(1, 2)
     ag_wait(1, 0)
     ag_wait(1, 1)
     back_hidden(0)
     ag_forward(1, 3)
-    rs_first(0)
+    rs_first(0, 3)
+    rs_first(0, 2)
     ag_wait(1, 2)
     ag_wait(1, 3)
     back_hidden(1)
@@ -378,22 +395,30 @@
     weight_grads(1)
     for copy in ys[1]:
         copy.start()
+    rs_pass_on(0, 3)
+    rs_first(0, 1)
     weight_grads(2)
     for copy in ys[2]:
         copy.start()
-    rs_pass_on(0, 0)
-    rs_pass_on(0, 1)
+    rs_pass_on(0, 2)
+    rs_first(0, 0)
     weight_grads(3)
     for c in range(CH):
         for copy in ag_copies(0, c):
             copy.wait_send()
+    back_tokens(1)
+    rs_first(1, 3)
+    rs_pass_on(0, 1)
     back_tokens(0)
-    back_tokens(1)
-    rs_first(1)
+    rs_pass_on(0, 0)
+    rs_first(1, 2)
     for k in range(2):
         for j in range(1, NE):
             z_copy(k, j).wait_send()
-    rs_last(0, 0)
+    rs_last(0, 3)
+    rs_last(0, 2)
+    rs_pass_on(1, 3)
+    rs_first(1, 1)
     for copy in ys[0]:
         copy.wait_recv()
     FH, HH = FB // 2, HID // 2
@@ -406,11 +431,17 @@
     ys[3][2].start()
     ys[3][3].start()
     rs_last(0, 1)
+    rs_pass_on(1, 2)
+    rs_first(1, 0)
+    rs_last(0, 0)
+    rs_last(1, 3)
+    rs_pass_on(1, 1)
+    rs_last(1, 2)
     rs_pass_on(1, 0)
-    rs_pass_on(1, 1)
+    rs_last(1, 1)
     rs_last(1, 0)
-    rs_last(1, 1)
-    mixed[...] = (weight[...] * back(0).astype(BF16).astype(F32)).astype(BF16)
+    mixed[...] = (weight * back(0).astype(BF16).astype(F32)).astype(BF16)
+    grad_tokens[...] = back(1).astype(BF16)
     for copy in ys[1] + ys[2] + ys[3]:
         copy.wait_recv()
     both = (
@@ -421,13 +452,12 @@
     out_down[0] = (
         g_dn[3].astype(F32) + y_left_dn[...].astype(F32) + y_right_dn[...].astype(F32)
     ).astype(BF16)
-    grad_tokens[...] = back(1).astype(BF16)
 
     for c in range(CH):
         for copy in ag_copies(1, c):
             copy.wait_send()
     for k in range(2):
-        for m in range(HALVES):
+        for m in range(CH):
             for copy in rs_copies(k, m):
                 copy.wait_send()
         for j in range(1, NE):
@@ -437,22 +467,47 @@
             copy.wait_send()
 
 
+def finish_kernel(*refs):
+    n = len(refs) // 2
+    sem = refs[-1]
+    copies = [pltpu.make_async_copy(refs[i], refs[n + i], sem.at[i]) for i in range(n)]
+    for copy in copies:
+        copy.start()
+    for copy in copies:
+        copy.wait()
+
+
+def finish(*parts):
+    far = pl.BlockSpec(memory_space=pl.ANY)
+    return pl.pallas_call(
+        finish_kernel,
+        out_shape=tuple(jax.ShapeDtypeStruct(p.shape, p.dtype) for p in parts),
+        in_specs=[pl.BlockSpec(memory_space=pltpu.VMEM)] * len(parts),
+        out_specs=(far,) * len(parts),
+        scratch_shapes=[pltpu.SemaphoreType.DMA((len(parts),))],
+        compiler_params=pltpu.CompilerParams(vmem_limit_bytes=2**20),
+        name="hand_over",
+    )(*parts)
+
+
 def body(tokens, expert_id, route_weight, cluster_id, out_grad, w_gate, w_up, w_down):
     vmem, far = pl.BlockSpec(memory_space=pltpu.VMEM), pl.BlockSpec(memory_space=pl.ANY)
     dma = pltpu.SemaphoreType.DMA
     rollouts = cluster_id.shape[0]
-    return pl.pallas_call(
+    parts = pl.pallas_call(
         kernel,
         out_shape=(
-            jax.ShapeDtypeStruct((TOK, FB), BF16),
-            jax.ShapeDtypeStruct((TOK, FB), BF16),
-            jax.ShapeDtypeStruct((1, FB, HID), BF16),
-            jax.ShapeDtypeStruct((1, FB, HID), BF16),
-            jax.ShapeDtypeStruct((1, HID, FB), BF16),
+            pltpu.VMEM((TOK, FB), BF16),
+            pltpu.VMEM((TOK, FB), BF16),
+            pltpu.VMEM((1, FB, HID), BF16),
+            pltpu.VMEM((1, FB, HID), BF16),
+            pltpu.VMEM((1, HID, FB), BF16),
         ),
-        in_specs=[vmem] * 7 + [far] * 3,
+        in_specs=[vmem] * 3 + [far] * 5,
         out_specs=(vmem,) * 5,
         scratch_shapes=[
+            pltpu.VMEM((TOK, FB), BF16),
+            pltpu.VMEM((TOK, FB), BF16),
             pltpu.VMEM((ROWS, FB), BF16),
             pltpu.VMEM((ROWS, FB), BF16),
             pltpu.VMEM((4, ROWS, FB), BF16),
@@ -465,7 +520,7 @@
             pltpu.VMEM((ROWS, HID), BF16),
             pltpu.VMEM((ROWS, 2 * HID), BF16),
             pltpu.VMEM((4, ROWS, FB), BF16),
-            pltpu.VMEM((2, HALVES, 2, QROWS, FB), BF16),
+            pltpu.VMEM((2, CH, 2, QROWS, FB), BF16),
             pltpu.VMEM((2, ROWS, FB), BF16),
             pltpu.VMEM((2, ROWS, FB), BF16),
             pltpu.VMEM((2, ROWS, FB), BF16),
@@ -477,34 +532,33 @@
             pltpu.VMEM((HID, FB), BF16),
             pltpu.VMEM((FB, 2 * HID), BF16),
             pltpu.VMEM((HID, FB), BF16),
-            dma((12,)),
+            dma((14,)),
             dma((2, NE)),
             dma((2, NE)),
             dma((2, CH, 4)),
             dma((2, CH, 4)),
-            dma((2, HALVES, 6)),
-            dma((2, HALVES, 6)),
+            dma((2, CH, 6)),
+            dma((2, CH, 6)),
             dma((2, NE)),
             dma((2, NE)),
             dma((12,)),
             dma((12,)),
         ],
         compiler_params=pltpu.CompilerParams(
-            collective_id=0, has_side_effects=True, vmem_limit_bytes=60 * 2**20
+            collective_id=0, has_side_effects=True, vmem_limit_bytes=LIMIT * 2**20
         ),
         name="expert_layer",
     )(
+        expert_id.reshape(1, TOK),
+        route_weight.reshape(1, TOK),
+        cluster_id.reshape(1, rollouts),
         tokens,
-        expert_id,
-        expert_id.reshape(1, TOK),
-        route_weight,
-        cluster_id.reshape(rollouts, 1),
-        cluster_id.reshape(1, rollouts),
         out_grad,
         w_gate,
         w_up,
         w_down,
     )
+    return finish(*parts)
 
 
 def solution(mesh):

time: 194 us -> 173 us (0.89)
  local copies, waits for them, and re-layouts: 11.5 us -> 0 us
  Pallas kernels: 180 us -> 170 us
    pallas_call x1 -> x2, Pallas kernels: 180 us -> 170 us  [the longest x1 169 us: body(): pl.pallas_call(kernel, out_shape=(pltpu.VMEM((TOK, FB), BF16), pltpu.VMEM...]
    unnamed x11 -> x0, local copies, waits for them, and re-layouts: 10.1 us -> none
where the time goes in v2:
time: 173 us; the launch traced here: 171 us
  Pallas kernels  170 us (98%)
    pallas_call x1, Pallas kernels, body(): pl.pallas_call(kernel, out_shape=(pltpu.VMEM((TOK, FB), BF16), pltpu.VMEM...  169 us

profile of v2, /device:TPU:9, one launch (start us, length us, event | category | flops | bytes accessed | tf_op | source)
XLA Modules:
  0.0 171.0 jit_solution(1840142903748274616)
XLA Ops:
  0.6 168.5 %expert_layer.1 = (bf16[128,1024]{1,0:T(8,128)(2,1)S(1)}, bf16[128,1024]{1,0:T(8,128)(2,1)S(1)}, bf16[1,1024,384]{2,1,0:T(8,128)(2,1)S(1)}, bf16[1,1024,384]{2,1,0:T(8,128)(2,1)S(1)}, bf16[1,384,1024]{2,1,0:T(8,128)(2,1)S(1)}) custom-call(s32[1,128]{1,0:T(1,128)} %bitcast.3, f32[1,128]{1,0:T(1,128)} %bitcast.4, s32[1,128]{1,0:T(1,128)} %bitcast.5, ...), custom_call_target="tpu_custom_call" | custom-call | tf_op jit(solution)/shard_map/expert_layer/pallas_call | solution.py:497
  169.2 1.6 hand_over.1

commit v3 on v2

v3 whole, which is shorter than its diff:
```python
import jax
import jax.numpy as jnp
from jax import lax
from jax.experimental import pallas as pl
from jax.experimental.pallas import tpu as pltpu
from jax.sharding import PartitionSpec as P

MESH = pl.DeviceIdType.MESH
F32, BF16 = jnp.float32, jnp.bfloat16
TOK = 128
CAP = 32
NE = 16
ROWS = NE * CAP
FB = 1024
HID = 384
GROUP = 16
LIMIT = 56
CH = 4
CROWS = ROWS // CH
HROWS = ROWS // 2
QROWS = CROWS // 2
FAR = (0, 1, 7, 2, 6, 3, 5, 4)


def dot_nn(a, b):
    return lax.dot_general(a, b, (((1,), (0,)), ((), ())), preferred_element_type=F32)


def dot_nt(a, b):
    return lax.dot_general(a, b, (((1,), (1,)), ((), ())), preferred_element_type=F32)


def dot_tn(a, b):
    return lax.dot_general(a, b, (((0,), (0,)), ((), ())), preferred_element_type=F32)


def kernel(
    eid_row,
    weight_row,
    clu_row,
    tokens_far,
    out_grad_far,
    w_gate,
    w_up,
    w_down,
    mixed,
    grad_tokens,
    out_gate,
    out_up,
    out_down,
    tokens,
    out_grad,
    send_t,
    send_c,
    rows_t,
    rows_c,
    wg,
    wu,
    wd,
    wdx,
    slope,
    silu,
    hid,
    gpy,
    rows_y,
    relay,
    acc,
    part_i,
    x_one,
    x_left,
    x_right,
    ret,
    g_dn,
    y_one,
    y_left,
    y_right,
    w_sem,
    z_ssem,
    z_rsem,
    ag_ssem,
    ag_rsem,
    rs_ssem,
    rs_rsem,
    zr_ssem,
    zr_rsem,
    wx_ssem,
    wx_rsem,
    wy_ssem,
    wy_rsem,
    ty_ssem,
    ty_rsem,
    hd_ssem,
    hd_rsem,
    gp_ssem,
    gp_rsem,
    y_ssem,
    y_rsem,
):
    x, y, e = lax.axis_index("tp"), lax.axis_index("rep"), lax.axis_index("exp")
    z, core = e // 2, e % 2
    x_next, x_prev = {"tp": (x + 1) % 4}, {"tp": (x + 3) % 4}
    y_next, y_prev = {"rep": (y + 1) % 4}, {"rep": (y + 3) % 4}
    x_far = {"tp": (x + 2) % 4}

    def to_of(j):
        return {"exp": ((z + FAR[j // 2]) % 8) * 2 + (core + j % 2) % 2}

    def from_of(j):
        return {"exp": ((z + 8 - FAR[j // 2]) % 8) * 2 + (core + j % 2) % 2}

    def remote(src, dst, ssem, rsem, where):
        return pltpu.make_async_remote_copy(
            src_ref=src,
            dst_ref=dst,
            send_sem=ssem,
            recv_sem=rsem,
            device_id=where,
            device_id_type=MESH,
        )

    barrier = pltpu.get_barrier_semaphore()
    for where in [to_of(j) for j in range(1, NE)] + [x_next, x_prev, x_far, y_next, y_prev]:
        pl.semaphore_signal(barrier, inc=1, device_id=where, device_id_type=MESH)
    load_t = pltpu.make_async_copy(tokens_far, tokens, w_sem.at[12])
    load_t.start()
    load_c = pltpu.make_async_copy(out_grad_far, out_grad, w_sem.at[13])
    load_c.start()

    loads, loads_d = [], []
    for i in range(4):
        at = pl.ds(pl.multiple_of(((x + i) % 4) * FB, FB), FB)
        loads.append(pltpu.make_async_copy(w_gate.at[0, at, :], wg.at[i], w_sem.at[i]))
        loads.append(pltpu.make_async_copy(w_up.at[0, at, :], wu.at[i], w_sem.at[4 + i]))
        loads_d.append(pltpu.make_async_copy(w_down.at[0, :, at], wd.at[i], w_sem.at[8 + i]))
    for load in loads_d + loads:
        load.start()

    def place(ids):
        away = ((ids >> 1) - z + 8) & 7
        first = jnp.where(away == 0, 0, jnp.where(away <= 4, 2 * away - 1, 16 - 2 * away))
        return (2 * first + (((ids & 1) + core) & 1)) * CAP

    sub = lax.broadcasted_iota(jnp.int32, (TOK, TOK), 0)
    lane = lax.broadcasted_iota(jnp.int32, (TOK, TOK), 1)

    def column(row):
        return jnp.sum(jnp.where(sub == lane, row, 0), axis=1, keepdims=True)

    ids_row = eid_row[...]
    ids_col = column(ids_row)
    same = ids_col == ids_row
    rank_col = jnp.sum(jnp.where(same & (lane < sub), 1.0, 0.0), axis=1, keepdims=True)
    rank_row = jnp.sum(jnp.where(same & (sub < lane), 1.0, 0.0), axis=0, keepdims=True)
    slot_col = place(ids_col) + rank_col.astype(jnp.int32)
    slot_row = place(ids_row) + rank_row.astype(jnp.int32)
    pick = jnp.where(
        lax.broadcasted_iota(jnp.int32, (ROWS, TOK), 0) == slot_row, 1.0, 0.0
    ).astype(BF16)
    load_t.wait()
    send_t[...] = dot_nn(pick, tokens[...]).astype(BF16)

    pl.semaphore_wait(barrier, NE - 1 + 5)

    def z_copy(k, j):
        src, dst = ((send_t, rows_t), (send_c, rows_c))[k]
        at = pl.ds(j * CAP, CAP)
        return remote(src.at[at], dst.at[0, at], z_ssem.at[k, j], z_rsem.at[k, j], to_of(j))

    def z_start(k, c):
        for j in range(max(4 * c, 1), 4 * c + 4):
            z_copy(k, j).start()

    z_start(0, 0)
    z_start(0, 1)
    rows_t[0, 0:CAP, :] = send_t[0:CAP, :]

    same_group = (sub // GROUP) == (lane // GROUP)
    votes = jnp.where((column(clu_row[...]) == clu_row[...]) & same_group, 1.0, 0.0)
    agree_row = jnp.sum(votes, axis=0, keepdims=True)
    agree_col = jnp.sum(votes, axis=1, keepdims=True)
    mean_row = jnp.sum(jnp.where(same_group, agree_col, 0.0), axis=0, keepdims=True) * (1.0 / GROUP)
    own = 2 * (y * NE + e) + sub // (TOK // 2)
    adv = jnp.sum(jnp.where(lane == own, agree_row - mean_row, 0.0), axis=1, keepdims=True)
    weight = column(weight_row[...])
    load_c.wait()
    cot = ((adv * weight) * out_grad[...].astype(F32)).astype(BF16)
    send_c[...] = dot_nn(pick, cot).astype(BF16)
    rows_c[0, 0:CAP, :] = send_c[0:CAP, :]

    def ring(buf, first, count, ssem, rsem, where, nxt, prv):
        lo = pl.ds(first, count)
        a, b = pl.ds(first, count // 2), pl.ds(first + count // 2, count // 2)
        s, r = [ssem.at[*where, n] for n in range(4)], [rsem.at[*where, n] for n in range(4)]
        return (
            remote(buf.at[0, lo], buf.at[3, lo], s[0], r[0], nxt),
            remote(buf.at[0, lo], buf.at[1, lo], s[1], r[1], prv),
            remote(buf.at[3, a], buf.at[2, a], s[2], r[2], nxt),
            remote(buf.at[1, b], buf.at[2, b], s[3], r[3], prv),
        )

    def ag_copies(k, c):
        buf = (rows_t, rows_c)[k]
        return ring(buf, c * CROWS, CROWS, ag_ssem, ag_rsem, (k, c), x_next, x_prev)

    def hd_copies(m):
        return ring(hid, m * HROWS, HROWS, hd_ssem, hd_rsem, (m,), x_next, x_prev)

    def gp_copies(m):
        return ring(gpy, m * HROWS, HROWS, gp_ssem, gp_rsem, (m,), y_next, y_prev)

    def begin(copies):
        for copy in copies[:2]:
            copy.start()

    def forward(copies):
        copies[0].wait_recv()
        copies[2].start()
        copies[1].wait_recv()
        copies[3].start()

    def ag_send(k, c):
        for j in range(max(4 * c, 1), 4 * c + 4):
            z_copy(k, j).wait_recv()
        for copy in ag_copies(k, c)[:2]:
            copy.start()

    def ag_forward(k, c):
        forward(ag_copies(k, c))

    def ag_wait(k, c):
        for copy in ag_copies(k, c)[2:]:
            copy.wait_recv()

    def hrows(m):
        return pl.ds(m * HROWS, HROWS)

    def first_layer(m):
        at = hrows(m)
        pre_g = dot_nn(rows_t[0, at, :], wg[0])
        for i in range(1, 4):
            pre_g += dot_nn(rows_t[i, at, :], wg[i])
        slope[at, :] = pre_g
        pre_u = dot_nn(rows_t[0, at, :], wu[0])
        for i in range(1, 4):
            pre_u += dot_nn(rows_t[i, at, :], wu[i])
        pre_g = slope[at, :]
        sig = jax.nn.sigmoid(pre_g)
        act = pre_g * sig
        hid[0, at, :] = (act * pre_u).astype(BF16)
        silu[at, :] = act
        slope[at, :] = pre_u * sig * (1.0 + pre_g * (1.0 - sig))

    QD = HID // 4

    def quarter(k, half=None):
        first = ((y + k) % 4) * QD
        if half is None:
            return pl.ds(pl.multiple_of(first, QD), QD)
        return pl.ds(pl.multiple_of(first + half * (QD // 2), QD // 2), QD // 2)

    def wx_copies():
        return [
            remote(
                wd.at[i, quarter(0)], wdx.at[3 - i, quarter(0)], wx_ssem.at[i - 1], wx_rsem.at[i - 1], where
            )
            for i, where in ((1, x_next), (2, x_far), (3, x_prev))
        ]

    def wy_copy(n, at, where):
        return remote(wdx.at[:, at], wdx.at[:, at], wy_ssem.at[n], wy_rsem.at[n], where)

    def wy_sends():
        return (
            wy_copy(0, quarter(0), y_next),
            wy_copy(1, quarter(0), y_prev),
            wy_copy(2, quarter(3, 0), y_next),
            wy_copy(3, quarter(1, 1), y_prev),
        )

    def wy_recvs():
        return (
            wy_copy(0, quarter(3), y_next),
            wy_copy(1, quarter(1), y_prev),
            wy_copy(2, quarter(2, 0), y_next),
            wy_copy(3, quarter(2, 1), y_prev),
        )

    def block(k):
        return (y + k - x + 4) % 4

    def ty_copies(m):
        lo = hrows(m)
        a, b = pl.ds(m * HROWS, HROWS // 2), pl.ds(m * HROWS + HROWS // 2, HROWS // 2)
        s, r = ty_ssem, ty_rsem
        return (
            remote(rows_t.at[block(2), a], relay.at[m, 0], s.at[m, 0], r.at[m, 0], y_next),
            remote(rows_t.at[block(2), b], relay.at[m, 1], s.at[m, 1], r.at[m, 1], y_prev),
            remote(rows_t.at[block(1), lo], rows_y.at[2, lo], s.at[m, 2], r.at[m, 2], y_next),
            remote(rows_t.at[block(3), lo], rows_y.at[0, lo], s.at[m, 3], r.at[m, 3], y_prev),
            remote(relay.at[m, 0], rows_y.at[1, a], s.at[m, 4], r.at[m, 4], y_next),
            remote(relay.at[m, 1], rows_y.at[1, b], s.at[m, 5], r.at[m, 5], y_prev),
        )

    def ty_first(m):
        for copy in ty_copies(m)[:4]:
            copy.start()

    def ty_forward(m):
        copies = ty_copies(m)
        for n in range(2):
            copies[n].wait_recv()
            copies[4 + n].start()

    def back_hidden(m):
        at = hrows(m)
        grad = dot_nt(rows_c[0, at, :], wd[0])
        for i in range(1, 4):
            grad += dot_nt(rows_c[i, at, :], wd[i])
        gpy[0, at, 0:HID] = (grad * slope[at, :]).astype(BF16)
        gpy[0, at, HID:] = (grad * silu[at, :]).astype(BF16)

    def back_tokens(m):
        @pl.loop(0, 4)
        def _(i):
            part_i[i, hrows(m), :] = (
                dot_nt(gpy[0, hrows(m), 0:HID], wg[i]) + dot_nt(gpy[0, hrows(m), HID:], wu[i])
            ).astype(BF16)

    ORDER = (2, 1, 3, 0)

    def down_grads(k):
        i = block(ORDER[k])

        @pl.loop(0, 4)
        def _(f):
            at = pl.ds(pl.multiple_of(f * 256, 256), 256)
            g_dn[k, :, at] = dot_tn(hid[0], rows_c[i, :, at]).astype(BF16)

    def gate_up_grads(k, last=False):
        rows = rows_t.at[block(0)] if k == 0 else rows_y.at[k - 1]

        @pl.loop(0, 4)
        def _(f):
            at = pl.ds(pl.multiple_of(f * 256, 256), 256)
            term = dot_tn(rows[:, at], gpy[k])
            if k == 0:
                acc[at, :] = term
            elif not last:
                acc[at, :] += term
            else:
                both = (acc[at, :] + term).astype(BF16)
                out_gate[0, at, :] = both[:, :HID]
                out_up[0, at, :] = both[:, HID:]

    def rs_copies(m):
        a, b = pl.ds(m * CROWS, QROWS), pl.ds(m * CROWS + QROWS, QROWS)
        s, r = rs_ssem, rs_rsem
        return (
            remote(part_i.at[2, a], x_one.at[m, 0], s.at[m, 0], r.at[m, 0], x_next),
            remote(part_i.at[2, b], x_one.at[m, 1], s.at[m, 1], r.at[m, 1], x_prev),
            remote(part_i.at[1, b], x_left.at[b], s.at[m, 2], r.at[m, 2], x_next),
            remote(part_i.at[3, a], x_right.at[a], s.at[m, 3], r.at[m, 3], x_prev),
            remote(part_i.at[1, a], x_left.at[a], s.at[m, 4], r.at[m, 4], x_next),
            remote(part_i.at[3, b], x_right.at[b], s.at[m, 5], r.at[m, 5], x_prev),
        )

    def add_into(ref, at, other):
        ref[at] = (ref[at].astype(F32) + other.astype(F32)).astype(BF16)

    def rs_first(m):
        for copy in rs_copies(m)[:4]:
            copy.start()

    def rs_pass_on(m):
        copies = rs_copies(m)
        copies[0].wait_recv()
        add_into(part_i, (1, pl.ds(m * CROWS, QROWS)), x_one[m, 0])
        copies[4].start()
        copies[1].wait_recv()
        add_into(part_i, (3, pl.ds(m * CROWS + QROWS, QROWS)), x_one[m, 1])
        copies[5].start()

    total = (send_t, send_c)

    def zr_copy(k, j):
        at = pl.ds(j * CAP, CAP)
        return remote(
            total[k].at[at], ret.at[k, at], zr_ssem.at[k, j], zr_rsem.at[k, j], from_of(j)
        )

    def zr_start(k, m):
        for j in range(max(m * 4, 1), m * 4 + 4):
            zr_copy(k, j).start()
        if m == 0:
            ret[k, 0:CAP, :] = total[k][0:CAP, :]

    def rs_last(m):
        for copy in rs_copies(m)[2:]:
            copy.wait_recv()
        at = pl.ds(m * CROWS, CROWS)
        total[1][at, :] = (
            part_i[0, at, :].astype(F32) + x_left[at, :].astype(F32) + x_right[at, :].astype(F32)
        ).astype(BF16)
        zr_start(1, m)

    def second_layer(m):
        for copy in hd_copies(m)[2:]:
            copy.wait_recv()
        at = hrows(m)
        out = dot_nn(hid[0, at, :], wd[0])
        for i in range(1, 4):
            out += dot_nn(hid[i, at, :], wdx[i - 1])
        total[0][at, :] = out.astype(BF16)
        zr_start(0, 2 * m + 1)
        zr_start(0, 2 * m)

    def back(k):
        for j in range(1, NE):
            zr_copy(k, j).wait_recv()
        spread = jnp.where(
            lax.broadcasted_iota(jnp.int32, (TOK, ROWS), 1) == slot_col, 1.0, 0.0
        ).astype(BF16)
        return dot_nn(spread, ret[k])

    HH = HID // 2
    dn_a, dn_b = pl.ds(0, HH), pl.ds(HH, HH)

    def y_copies():
        s, r = y_ssem, y_rsem
        return (
            remote(g_dn.at[0, dn_a], y_one.at[0], s.at[0], r.at[0], y_next),
            remote(g_dn.at[0, dn_b], y_one.at[1], s.at[1], r.at[1], y_prev),
            remote(g_dn.at[1, dn_b], y_left.at[dn_b], s.at[2], r.at[2], y_next),
            remote(g_dn.at[2, dn_a], y_right.at[dn_a], s.at[3], r.at[3], y_prev),
            remote(g_dn.at[1, dn_a], y_left.at[dn_a], s.at[4], r.at[4], y_next),
            remote(g_dn.at[2, dn_b], y_right.at[dn_b], s.at[5], r.at[5], y_prev),
        )

    for load in loads_d:
        load.wait()
    for copy in wx_copies():
        copy.start()
    ag_send(0, 0)
    z_start(0, 2)
    ag_send(0, 1)
    z_start(0, 3)
    ag_forward(0, 0)
    ag_send(0, 2)
    z_start(1, 0)
    z_start(1, 1)
    for copy in wx_copies():
        copy.wait_recv()
    begin(wy_sends())
    ag_forward(0, 1)
    ag_send(0, 3)
    z_start(1, 2)
    ag_forward(0, 2)
    z_start(1, 3)
    ag_send(1, 0)
    ag_forward(0, 3)
    ag_send(1, 1)
    for load in loads:
        load.wait()
    ag_wait(0, 0)
    ag_wait(0, 1)
    ty_first(0)
    first_layer(0)
    for n in range(2):
        wy_recvs()[n].wait_recv()
        wy_sends()[2 + n].start()
    ag_send(1, 2)
    ag_forward(1, 0)
    ag_send(1, 3)
    ag_wait(0, 2)
    ag_wait(0, 3)
    ty_first(1)
    first_layer(1)
    ag_forward(1, 1)
    ty_forward(0)
    ag_forward(1, 2)
    ag_wait(1, 0)
    ag_wait(1, 1)
    back_hidden(0)
    begin(gp_copies(0))
    ag_forward(1, 3)
    begin(hd_copies(1))
    begin(hd_copies(0))
    ty_forward(1)
    ag_wait(1, 2)
    ag_wait(1, 3)
    back_hidden(1)
    begin(gp_copies(1))
    ys = y_copies()
    down_grads(0)
    ys[0].start()
    ys[1].start()
    down_grads(1)
    ys[2].start()
    down_grads(2)
    ys[3].start()
    back_tokens(1)
    rs_first(3)
    rs_first(2)
    forward(hd_copies(1))
    forward(hd_copies(0))
    back_tokens(0)
    forward(gp_copies(0))
    rs_pass_on(3)
    rs_first(1)
    for copy in wy_recvs()[2:]:
        copy.wait_recv()
    for k in range(2):
        for j in range(1, NE):
            z_copy(k, j).wait_send()
    second_layer(1)
    rs_pass_on(2)
    rs_first(0)
    second_layer(0)
    forward(gp_copies(1))
    ys[0].wait_recv()
    add_into(g_dn, (1, dn_a), y_one[0])
    ys[4].start()
    ys[1].wait_recv()
    add_into(g_dn, (2, dn_b), y_one[1])
    ys[5].start()
    gate_up_grads(0)
    rs_pass_on(1)
    rs_last(3)
    for m in range(2):
        ty_copies(m)[2].wait_recv()
        ty_copies(m)[3].wait_recv()
    gate_up_grads(3)
    rs_pass_on(0)
    rs_last(2)
    gate_up_grads(1)
    down_grads(3)
    rs_last(1)
    rs_last(0)
    mixed[...] = (weight * back(0).astype(BF16).astype(F32)).astype(BF16)
    for m in range(2):
        ty_copies(m)[4].wait_recv()
        ty_copies(m)[5].wait_recv()
        gp_copies(m)[2].wait_recv()
        gp_copies(m)[3].wait_recv()
    gate_up_grads(2, last=True)
    for copy in ys[2:]:
        copy.wait_recv()
    out_down[0] = (
        g_dn[3].astype(F32) + y_left[...].astype(F32) + y_right[...].astype(F32)
    ).astype(BF16)
    grad_tokens[...] = back(1).astype(BF16)

    for k in range(2):
        for c in range(CH):
            for copy in ag_copies(k, c):
                copy.wait_send()
        for copy in ty_copies(k) + hd_copies(k) + gp_copies(k):
            copy.wait_send()
        for j in range(1, NE):
            zr_copy(k, j).wait_send()
    for m in range(CH):
        for copy in rs_copies(m):
            copy.wait_send()
    for copy in wx_copies() + list(wy_sends()) + list(ys):
        copy.wait_send()


def finish_kernel(*refs):
    n = len(refs) // 2
    sem = refs[-1]
    copies = [pltpu.make_async_copy(refs[i], refs[n + i], sem.at[i]) for i in range(n)]
    for copy in copies:
        copy.start()
    for copy in copies:
        copy.wait()


def finish(*parts):
    far = pl.BlockSpec(memory_space=pl.ANY)
    return pl.pallas_call(
        finish_kernel,
        out_shape=tuple(jax.ShapeDtypeStruct(p.shape, p.dtype) for p in parts),
        in_specs=[pl.BlockSpec(memory_space=pltpu.VMEM)] * len(parts),
        out_specs=(far,) * len(parts),
        scratch_shapes=[pltpu.SemaphoreType.DMA((len(parts),))],
        compiler_params=pltpu.CompilerParams(vmem_limit_bytes=2**20),
        name="hand_over",
    )(*parts)


def body(tokens, expert_id, route_weight, cluster_id, out_grad, w_gate, w_up, w_down):
    vmem, far = pl.BlockSpec(memory_space=pltpu.VMEM), pl.BlockSpec(memory_space=pl.ANY)
    dma = pltpu.SemaphoreType.DMA
    rollouts = cluster_id.shape[0]
    parts = pl.pallas_call(
        kernel,
        out_shape=(
            pltpu.VMEM((TOK, FB), BF16),
            pltpu.VMEM((TOK, FB), BF16),
            pltpu.VMEM((1, FB, HID), BF16),
            pltpu.VMEM((1, FB, HID), BF16),
            pltpu.VMEM((1, HID, FB), BF16),
        ),
        in_specs=[vmem] * 3 + [far] * 5,
        out_specs=(vmem,) * 5,
        scratch_shapes=[
            pltpu.VMEM((TOK, FB), BF16),
            pltpu.VMEM((TOK, FB), BF16),
            pltpu.VMEM((ROWS, FB), BF16),
            pltpu.VMEM((ROWS, FB), BF16),
            pltpu.VMEM((4, ROWS, FB), BF16),
            pltpu.VMEM((4, ROWS, FB), BF16),
            pltpu.VMEM((4, FB, HID), BF16),
            pltpu.VMEM((4, FB, HID), BF16),
            pltpu.VMEM((4, HID, FB), BF16),
            pltpu.VMEM((3, HID, FB), BF16),
            pltpu.VMEM((ROWS, HID), F32),
            pltpu.VMEM((ROWS, HID), F32),
            pltpu.VMEM((4, ROWS, HID), BF16),
            pltpu.VMEM((4, ROWS, 2 * HID), BF16),
            pltpu.VMEM((3, ROWS, FB), BF16),
            pltpu.VMEM((2, 2, HROWS // 2, FB), BF16),
            pltpu.VMEM((FB, 2 * HID), F32),
            pltpu.VMEM((4, ROWS, FB), BF16),
            pltpu.VMEM((CH, 2, QROWS, FB), BF16),
            pltpu.VMEM((ROWS, FB), BF16),
            pltpu.VMEM((ROWS, FB), BF16),
            pltpu.VMEM((2, ROWS, FB), BF16),
            pltpu.VMEM((4, HID, FB), BF16),
            pltpu.VMEM((2, HID // 2, FB), BF16),
            pltpu.VMEM((HID, FB), BF16),
            pltpu.VMEM((HID, FB), BF16),
            dma((14,)),
            dma((2, NE)),
            dma((2, NE)),
            dma((2, CH, 4)),
            dma((2, CH, 4)),
            dma((CH, 6)),
            dma((CH, 6)),
            dma((2, NE)),
            dma((2, NE)),
            dma((3,)),
            dma((3,)),
            dma((4,)),
            dma((4,)),
            dma((2, 6)),
            dma((2, 6)),
            dma((2, 4)),
            dma((2, 4)),
            dma((2, 4)),
            dma((2, 4)),
            dma((6,)),
            dma((6,)),
        ],
        compiler_params=pltpu.CompilerParams(
            collective_id=0, has_side_effects=True, vmem_limit_bytes=LIMIT * 2**20
        ),
        name="expert_layer",
    )(
        expert_id.reshape(1, TOK),
        route_weight.reshape(1, TOK),
        cluster_id.reshape(1, rollouts),
        tokens,
        out_grad,
        w_gate,
        w_up,
        w_down,
    )
    return finish(*parts)


def solution(mesh):
    placed = (
        P(("rep", "exp"), "tp"),
        P(("rep", "exp"), None),
        P(("rep", "exp"), None),
        P(),
        P(("rep", "exp"), "tp"),
        P("exp", None, "tp"),
        P("exp", None, "tp"),
        P("exp", "tp", None),
    )
    return jax.shard_map(
        body,
        mesh=mesh,
        in_specs=placed,
        out_specs=(
            P(("rep", "exp"), "tp"),
            P(("rep", "exp"), "tp"),
            P("exp", "rep", "tp"),
            P("exp", "rep", "tp"),
            P("exp", "tp", "rep"),
        ),
        check_vma=False,
    )
```

time: 173 us -> 168 us (0.971)
  Pallas kernels: 170 us -> 167 us
    pallas_call x1, Pallas kernels: 169 us -> 165 us  [body(): pl.pallas_call(kernel, out_shape=(pltpu.VMEM((TOK, FB), BF16), pltpu.VMEM...]
where the time goes in v3:
time: 168 us
  Pallas kernels  167 us (99%)
    pallas_call x1, Pallas kernels, body(): pl.pallas_call(kernel, out_shape=(pltpu.VMEM((TOK, FB), BF16), pltpu.VMEM...  165 us

profile of v3, /device:TPU:9, one launch (start us, length us, event | category | flops | bytes accessed | tf_op | source)
XLA Modules:
  0.0 167.6 jit_solution(11358937604103794493)
XLA Ops:
  0.6 165.2 %expert_layer.1 = (bf16[128,1024]{1,0:T(8,128)(2,1)S(1)}, bf16[128,1024]{1,0:T(8,128)(2,1)S(1)}, bf16[1,1024,384]{2,1,0:T(8,128)(2,1)S(1)}, bf16[1,1024,384]{2,1,0:T(8,128)(2,1)S(1)}, bf16[1,384,1024]{2,1,0:T(8,128)(2,1)S(1)}) custom-call(s32[1,128]{1,0:T(1,128)} %bitcast.3, f32[1,128]{1,0:T(1,128)} %bitcast.4, s32[1,128]{1,0:T(1,128)} %bitcast.5, ...), custom_call_target="tpu_custom_call" | custom-call | tf_op jit(solution)/shard_map/expert_layer/pallas_call | solution.py:595
  165.9 1.6 hand_over.1

commit v4 on v3

--- a/solution.py
+++ b/solution.py
@@ -19,7 +19,7 @@
 CROWS = ROWS // CH
 HROWS = ROWS // 2
 QROWS = CROWS // 2
-FAR = (0, 1, 7, 2, 6, 3, 5, 4)
+FAR = (0, 1, 3, 5, 4, 7, 2, 6)
 
 
 def dot_nn(a, b):
@@ -137,7 +137,7 @@
 
     def place(ids):
         away = ((ids >> 1) - z + 8) & 7
-        first = jnp.where(away == 0, 0, jnp.where(away <= 4, 2 * away - 1, 16 - 2 * away))
+        first = sum(jnp.where(away == far, n, 0) for n, far in enumerate(FAR))
         return (2 * first + (((ids & 1) + core) & 1)) * CAP
 
     sub = lax.broadcasted_iota(jnp.int32, (TOK, TOK), 0)
@@ -289,8 +289,8 @@
         return (y + k - x + 4) % 4
 
     def ty_copies(m):
-        lo = hrows(m)
-        a, b = pl.ds(m * HROWS, HROWS // 2), pl.ds(m * HROWS + HROWS // 2, HROWS // 2)
+        lo = pl.ds(m * CROWS, CROWS)
+        a, b = pl.ds(m * CROWS, QROWS), pl.ds(m * CROWS + QROWS, QROWS)
         s, r = ty_ssem, ty_rsem
         return (
             remote(rows_t.at[block(2), a], relay.at[m, 0], s.at[m, 0], r.at[m, 0], y_next),
@@ -302,6 +302,7 @@
         )
 
     def ty_first(m):
+        ag_wait(0, m)
         for copy in ty_copies(m)[:4]:
             copy.start()
 
@@ -452,94 +453,95 @@
         copy.wait_recv()
     begin(wy_sends())
     ag_forward(0, 1)
+    ty_first(0)
     ag_send(0, 3)
     z_start(1, 2)
     ag_forward(0, 2)
+    ty_first(1)
     z_start(1, 3)
     ag_send(1, 0)
     ag_forward(0, 3)
+    for n in range(2):
+        wy_recvs()[n].wait_recv()
+        wy_sends()[2 + n].start()
+    ty_first(2)
+    ty_forward(0)
     ag_send(1, 1)
     for load in loads:
         load.wait()
-    ag_wait(0, 0)
-    ag_wait(0, 1)
-    ty_first(0)
     first_layer(0)
-    for n in range(2):
-        wy_recvs()[n].wait_recv()
-        wy_sends()[2 + n].start()
+    begin(hd_copies(0))
     ag_send(1, 2)
     ag_forward(1, 0)
     ag_send(1, 3)
-    ag_wait(0, 2)
-    ag_wait(0, 3)
-    ty_first(1)
+    ty_first(3)
+    ty_forward(1)
     first_layer(1)
     ag_forward(1, 1)
-    ty_forward(0)
+    ty_forward(2)
+    forward(hd_copies(0))
     ag_forward(1, 2)
     ag_wait(1, 0)
     ag_wait(1, 1)
     back_hidden(0)
     begin(gp_copies(0))
+    for k in range(2):
+        for j in range(1, NE):
+            z_copy(k, j).wait_send()
+    for copy in wy_recvs()[2:]:
+        copy.wait_recv()
+    second_layer(0)
+    ty_forward(3)
     ag_forward(1, 3)
     begin(hd_copies(1))
-    begin(hd_copies(0))
-    ty_forward(1)
     ag_wait(1, 2)
     ag_wait(1, 3)
     back_hidden(1)
     begin(gp_copies(1))
+    forward(hd_copies(1))
+    back_tokens(1)
+    rs_first(3)
+    rs_first(2)
     ys = y_copies()
     down_grads(0)
     ys[0].start()
     ys[1].start()
+    forward(gp_copies(0))
     down_grads(1)
     ys[2].start()
     down_grads(2)
     ys[3].start()
-    back_tokens(1)
-    rs_first(3)
-    rs_first(2)
-    forward(hd_copies(1))
-    forward(hd_copies(0))
     back_tokens(0)
-    forward(gp_copies(0))
     rs_pass_on(3)
     rs_first(1)
-    for copy in wy_recvs()[2:]:
-        copy.wait_recv()
-    for k in range(2):
-        for j in range(1, NE):
-            z_copy(k, j).wait_send()
     second_layer(1)
     rs_pass_on(2)
     rs_first(0)
-    second_layer(0)
+    gate_up_grads(0)
     forward(gp_copies(1))
+    rs_last(3)
     ys[0].wait_recv()
     add_into(g_dn, (1, dn_a), y_one[0])
     ys[4].start()
     ys[1].wait_recv()
     add_into(g_dn, (2, dn_b), y_one[1])
     ys[5].start()
-    gate_up_grads(0)
     rs_pass_on(1)
-    rs_last(3)
-    for m in range(2):
+    for m in range(CH):
         ty_copies(m)[2].wait_recv()
         ty_copies(m)[3].wait_recv()
     gate_up_grads(3)
-    rs_pass_on(0)
     rs_last(2)
     gate_up_grads(1)
+    rs_pass_on(0)
     down_grads(3)
+    mixed[...] = (weight * back(0).astype(BF16).astype(F32)).astype(BF16)
     rs_last(1)
     rs_last(0)
-    mixed[...] = (weight * back(0).astype(BF16).astype(F32)).astype(BF16)
-    for m in range(2):
+    for m in range(CH):
         ty_copies(m)[4].wait_recv()
         ty_copies(m)[5].wait_recv()
+    for m in range(2):
         gp_copies(m)[2].wait_recv()
         gp_copies(m)[3].wait_recv()
     gate_up_grads(2, last=True)
@@ -554,12 +556,12 @@
         for c in range(CH):
             for copy in ag_copies(k, c):
                 copy.wait_send()
-        for copy in ty_copies(k) + hd_copies(k) + gp_copies(k):
+        for copy in hd_copies(k) + gp_copies(k):
             copy.wait_send()
         for j in range(1, NE):
             zr_copy(k, j).wait_send()
     for m in range(CH):
-        for copy in rs_copies(m):
+        for copy in ty_copies(m) + rs_copies(m):
             copy.wait_send()
     for copy in wx_copies() + list(wy_sends()) + list(ys):
         copy.wait_send()
@@ -619,7 +621,7 @@
             pltpu.VMEM((4, ROWS, HID), BF16),
             pltpu.VMEM((4, ROWS, 2 * HID), BF16),
             pltpu.VMEM((3, ROWS, FB), BF16),
-            pltpu.VMEM((2, 2, HROWS // 2, FB), BF16),
+            pltpu.VMEM((CH, 2, QROWS, FB), BF16),
             pltpu.VMEM((FB, 2 * HID), F32),
             pltpu.VMEM((4, ROWS, FB), BF16),
             pltpu.VMEM((CH, 2, QROWS, FB), BF16),
@@ -643,8 +645,8 @@
             dma((3,)),
             dma((4,)),
             dma((4,)),
-            dma((2, 6)),
-            dma((2, 6)),
+            dma((CH, 6)),
+            dma((CH, 6)),
             dma((2, 4)),
             dma((2, 4)),
             dma((2, 4)),

time: 168 us -> 157 us (0.935)
  Pallas kernels: 167 us -> 156 us
    pallas_call x1, Pallas kernels: 165 us -> 154 us  [body(): pl.pallas_call(kernel, out_shape=(pltpu.VMEM((TOK, FB), BF16), pltpu.VMEM...]
where the time goes in v4:
time: 157 us
  Pallas kernels  156 us (99%)
    pallas_call x1, Pallas kernels, body(): pl.pallas_call(kernel, out_shape=(pltpu.VMEM((TOK, FB), BF16), pltpu.VMEM...  154 us

profile of v4, /device:TPU:9, one launch (start us, length us, event | category | flops | bytes accessed | tf_op | source)
XLA Modules:
  0.0 156.9 jit_solution(15290684767758763904)
XLA Ops:
  0.6 154.5 %expert_layer.1 = (bf16[128,1024]{1,0:T(8,128)(2,1)S(1)}, bf16[128,1024]{1,0:T(8,128)(2,1)S(1)}, bf16[1,1024,384]{2,1,0:T(8,128)(2,1)S(1)}, bf16[1,1024,384]{2,1,0:T(8,128)(2,1)S(1)}, bf16[1,384,1024]{2,1,0:T(8,128)(2,1)S(1)}) custom-call(s32[1,128]{1,0:T(1,128)} %bitcast.3, f32[1,128]{1,0:T(1,128)} %bitcast.4, s32[1,128]{1,0:T(1,128)} %bitcast.5, ...), custom_call_target="tpu_custom_call" | custom-call | tf_op jit(solution)/shard_map/expert_layer/pallas_call | solution.py:597
  155.1 1.6 %hand_over.1 = (bf16[128,1024]{1,0:T(8,128)(2,1)}, bf16[128,1024]{1,0:T(8,128)(2,1)}, bf16[1,1024,384]{2,1,0:T(8,128)(2,1)}, bf16[1,1024,384]{2,1,0:T(8,128)(2,1)}, bf16[1,384,1024]{2,1,0:T(8,128)(2,1)}) custom-call(bf16[128,1024]{1,0:T(8,128)(2,1)S(1)} %get-tuple-element.10.refs_0_, bf16[128,1024]{1,0:T(8,128)(2,1)S(1)} %get-tuple-element.11.refs_1_, ...), custom_call_target="tpu_custom_call" | custom-call | tf_op jit(solution)/shard_map/hand_over/pallas_call | solution.py:582

commit v5 on v4

--- a/solution.py
+++ b/solution.py
@@ -174,18 +174,20 @@
     z_start(0, 1)
     rows_t[0, 0:CAP, :] = send_t[0:CAP, :]
 
-    same_group = (sub // GROUP) == (lane // GROUP)
-    votes = jnp.where((column(clu_row[...]) == clu_row[...]) & same_group, 1.0, 0.0)
-    agree_row = jnp.sum(votes, axis=0, keepdims=True)
-    agree_col = jnp.sum(votes, axis=1, keepdims=True)
-    mean_row = jnp.sum(jnp.where(same_group, agree_col, 0.0), axis=0, keepdims=True) * (1.0 / GROUP)
-    own = 2 * (y * NE + e) + sub // (TOK // 2)
-    adv = jnp.sum(jnp.where(lane == own, agree_row - mean_row, 0.0), axis=1, keepdims=True)
     weight = column(weight_row[...])
-    load_c.wait()
-    cot = ((adv * weight) * out_grad[...].astype(F32)).astype(BF16)
-    send_c[...] = dot_nn(pick, cot).astype(BF16)
-    rows_c[0, 0:CAP, :] = send_c[0:CAP, :]
+
+    def make_cotangent():
+        same_group = (sub // GROUP) == (lane // GROUP)
+        votes = jnp.where((column(clu_row[...]) == clu_row[...]) & same_group, 1.0, 0.0)
+        agree_row = jnp.sum(votes, axis=0, keepdims=True)
+        agree_col = jnp.sum(votes, axis=1, keepdims=True)
+        mean_row = jnp.sum(jnp.where(same_group, agree_col, 0.0), axis=0, keepdims=True) * (1.0 / GROUP)
+        own = 2 * (y * NE + e) + sub // (TOK // 2)
+        adv = jnp.sum(jnp.where(lane == own, agree_row - mean_row, 0.0), axis=1, keepdims=True)
+        load_c.wait()
+        cot = ((adv * weight) * out_grad[...].astype(F32)).astype(BF16)
+        send_c[...] = dot_nn(pick, cot).astype(BF16)
+        rows_c[0, 0:CAP, :] = send_c[0:CAP, :]
 
     def ring(buf, first, count, ssem, rsem, where, nxt, prv):
         lo = pl.ds(first, count)
@@ -312,19 +314,21 @@
             copies[n].wait_recv()
             copies[4 + n].start()
 
-    def back_hidden(m):
-        at = hrows(m)
+    def back_hidden(first, count):
+        at = pl.ds(first, count)
         grad = dot_nt(rows_c[0, at, :], wd[0])
         for i in range(1, 4):
             grad += dot_nt(rows_c[i, at, :], wd[i])
         gpy[0, at, 0:HID] = (grad * slope[at, :]).astype(BF16)
         gpy[0, at, HID:] = (grad * silu[at, :]).astype(BF16)
 
-    def back_tokens(m):
+    def back_tokens(first, count):
+        at = pl.ds(first, count)
+
         @pl.loop(0, 4)
         def _(i):
-            part_i[i, hrows(m), :] = (
-                dot_nt(gpy[0, hrows(m), 0:HID], wg[i]) + dot_nt(gpy[0, hrows(m), HID:], wu[i])
+            part_i[i, at, :] = (
+                dot_nt(gpy[0, at, 0:HID], wg[i]) + dot_nt(gpy[0, at, HID:], wu[i])
             ).astype(BF16)
 
     ORDER = (2, 1, 3, 0)
@@ -443,15 +447,16 @@
         copy.start()
     ag_send(0, 0)
     z_start(0, 2)
+    make_cotangent()
     ag_send(0, 1)
     z_start(0, 3)
+    for copy in wx_copies():
+        copy.wait_recv()
+    begin(wy_sends())
     ag_forward(0, 0)
     ag_send(0, 2)
     z_start(1, 0)
     z_start(1, 1)
-    for copy in wx_copies():
-        copy.wait_recv()
-    begin(wy_sends())
     ag_forward(0, 1)
     ty_first(0)
     ag_send(0, 3)
@@ -483,7 +488,7 @@
     ag_forward(1, 2)
     ag_wait(1, 0)
     ag_wait(1, 1)
-    back_hidden(0)
+    back_hidden(0, HROWS)
     begin(gp_copies(0))
     for k in range(2):
         for j in range(1, NE):
@@ -491,32 +496,36 @@
     for copy in wy_recvs()[2:]:
         copy.wait_recv()
     second_layer(0)
+    back_tokens(0, HROWS)
     ty_forward(3)
     ag_forward(1, 3)
     begin(hd_copies(1))
+    rs_first(1)
     ag_wait(1, 2)
+    back_hidden(2 * CROWS, CROWS)
     ag_wait(1, 3)
-    back_hidden(1)
+    back_hidden(3 * CROWS, CROWS)
     begin(gp_copies(1))
-    forward(hd_copies(1))
-    back_tokens(1)
-    rs_first(3)
-    rs_first(2)
     ys = y_copies()
     down_grads(0)
     ys[0].start()
     ys[1].start()
+    forward(hd_copies(1))
+    back_tokens(3 * CROWS, CROWS)
+    rs_first(3)
+    rs_pass_on(1)
+    back_tokens(2 * CROWS, CROWS)
+    rs_first(2)
+    second_layer(1)
     forward(gp_copies(0))
     down_grads(1)
     ys[2].start()
     down_grads(2)
     ys[3].start()
-    back_tokens(0)
     rs_pass_on(3)
-    rs_first(1)
-    second_layer(1)
+    rs_first(0)
     rs_pass_on(2)
-    rs_first(0)
+    rs_last(1)
     gate_up_grads(0)
     forward(gp_copies(1))
     rs_last(3)
@@ -526,18 +535,16 @@
     ys[1].wait_recv()
     add_into(g_dn, (2, dn_b), y_one[1])
     ys[5].start()
-    rs_pass_on(1)
+    rs_pass_on(0)
     for m in range(CH):
         ty_copies(m)[2].wait_recv()
         ty_copies(m)[3].wait_recv()
     gate_up_grads(3)
     rs_last(2)
     gate_up_grads(1)
-    rs_pass_on(0)
+    rs_last(0)
     down_grads(3)
     mixed[...] = (weight * back(0).astype(BF16).astype(F32)).astype(BF16)
-    rs_last(1)
-    rs_last(0)
     for m in range(CH):
         ty_copies(m)[4].wait_recv()
         ty_copies(m)[5].wait_recv()

time: 157 us -> 155 us (0.987); the launches traced: 157 us -> 153 us
  Pallas kernels: 156 us -> 152 us
    pallas_call x1, Pallas kernels: 154 us -> 151 us  [body(): pl.pallas_call(kernel, out_shape=(pltpu.VMEM((TOK, FB), BF16), pltpu.VMEM...]
where the time goes in v5:
time: 155 us; the launch traced here: 153 us
  Pallas kernels  152 us (98%)
    pallas_call x1, Pallas kernels, body(): pl.pallas_call(kernel, out_shape=(pltpu.VMEM((TOK, FB), BF16), pltpu.VMEM...  151 us

profile of v5, /device:TPU:9, one launch (start us, length us, event | category | flops | bytes accessed | tf_op | source)
XLA Modules:
  0.0 153.0 jit_solution(11018266442544997252)
XLA Ops:
  0.6 150.5 %expert_layer.1 = (bf16[128,1024]{1,0:T(8,128)(2,1)S(1)}, bf16[128,1024]{1,0:T(8,128)(2,1)S(1)}, bf16[1,1024,384]{2,1,0:T(8,128)(2,1)S(1)}, bf16[1,1024,384]{2,1,0:T(8,128)(2,1)S(1)}, bf16[1,384,1024]{2,1,0:T(8,128)(2,1)S(1)}) custom-call(s32[1,128]{1,0:T(1,128)} %bitcast.3, f32[1,128]{1,0:T(1,128)} %bitcast.4, s32[1,128]{1,0:T(1,128)} %bitcast.5, ...), custom_call_target="tpu_custom_call" | custom-call | tf_op jit(solution)/shard_map/expert_layer/pallas_call | solution.py:604
  151.2 1.6 %hand_over.1 = (bf16[128,1024]{1,0:T(8,128)(2,1)}, bf16[128,1024]{1,0:T(8,128)(2,1)}, bf16[1,1024,384]{2,1,0:T(8,128)(2,1)}, bf16[1,1024,384]{2,1,0:T(8,128)(2,1)}, bf16[1,384,1024]{2,1,0:T(8,128)(2,1)}) custom-call(bf16[128,1024]{1,0:T(8,128)(2,1)S(1)} %get-tuple-element.10.refs_0_, bf16[128,1024]{1,0:T(8,128)(2,1)S(1)} %get-tuple-element.11.refs_1_, ...), custom_call_target="tpu_custom_call" | custom-call | tf_op jit(solution)/shard_map/hand_over/pallas_call | solution.py:589

commit v6 on v5

--- a/solution.py
+++ b/solution.py
@@ -157,7 +157,7 @@
         lax.broadcasted_iota(jnp.int32, (ROWS, TOK), 0) == slot_row, 1.0, 0.0
     ).astype(BF16)
     load_t.wait()
-    send_t[...] = dot_nn(pick, tokens[...]).astype(BF16)
+    send_t[0:CROWS, :] = dot_nn(pick[0:CROWS], tokens[...]).astype(BF16)
 
     pl.semaphore_wait(barrier, NE - 1 + 5)
 
@@ -171,6 +171,7 @@
             z_copy(k, j).start()
 
     z_start(0, 0)
+    send_t[CROWS:, :] = dot_nn(pick[CROWS:], tokens[...]).astype(BF16)
     z_start(0, 1)
     rows_t[0, 0:CAP, :] = send_t[0:CAP, :]
 

time: 155 us -> 155 us (level)
  no operation moved by 1% of the time
where the time goes in v6:
time: 155 us; the launch traced here: 154 us
  Pallas kernels  153 us (99%)
    pallas_call x1, Pallas kernels, body(): pl.pallas_call(kernel, out_shape=(pltpu.VMEM((TOK, FB), BF16), pltpu.VMEM...  152 us

profile of v6, /device:TPU:9, one launch (start us, length us, event | category | flops | bytes accessed | tf_op | source)
XLA Modules:
  0.0 154.2 jit_solution(3892711209057502216)
XLA Ops:
  0.6 151.8 %expert_layer.1 = (bf16[128,1024]{1,0:T(8,128)(2,1)S(1)}, bf16[128,1024]{1,0:T(8,128)(2,1)S(1)}, bf16[1,1024,384]{2,1,0:T(8,128)(2,1)S(1)}, bf16[1,1024,384]{2,1,0:T(8,128)(2,1)S(1)}, bf16[1,384,1024]{2,1,0:T(8,128)(2,1)S(1)}) custom-call(s32[1,128]{1,0:T(1,128)} %bitcast.3, f32[1,128]{1,0:T(1,128)} %bitcast.4, s32[1,128]{1,0:T(1,128)} %bitcast.5, ...), custom_call_target="tpu_custom_call" | custom-call | tf_op jit(solution)/shard_map/expert_layer/pallas_call | solution.py:605
  152.4 1.6 %hand_over.1 = (bf16[128,1024]{1,0:T(8,128)(2,1)}, bf16[128,1024]{1,0:T(8,128)(2,1)}, bf16[1,1024,384]{2,1,0:T(8,128)(2,1)}, bf16[1,1024,384]{2,1,0:T(8,128)(2,1)}, bf16[1,384,1024]{2,1,0:T(8,128)(2,1)}) custom-call(bf16[128,1024]{1,0:T(8,128)(2,1)S(1)} %get-tuple-element.10.refs_0_, bf16[128,1024]{1,0:T(8,128)(2,1)S(1)} %get-tuple-element.11.refs_1_, ...), custom_call_target="tpu_custom_call" | custom-call | tf_op jit(solution)/shard_map/hand_over/pallas_call | solution.py:590
